TPU v7x, 32 devices: a whole 2x2x4 slice. The times are simulated.
32 devices in a mesh: blk: 8 (over z, x), tm: 4 (over y, core).
Axes of the slice: x: 2, y: 2, z: 4, core: 2. Of those that a mesh axis runs over, the one named last changes fastest.
Arguments:
- density: bfloat16 [768, 256, 128], P('blk', 'tm'), may hold values from 0.5 to 2
- flow_rest: bfloat16 [768, 4, 256, 128], P('blk', None, 'tm'), may hold values from -6 to 6
- dest: int32 [768, 1], P('blk'), may hold values from 0 to 7; in each aligned block of 96 rows (0 to 95, 96 to 191, ...) at most 24 rows name the same one
- weights: bfloat16 [8, 64, 256, 128], P('blk', None, 'tm'), may hold values from -0.0024414062 to 0.0024414062
- directions: float32 [64, 3], replicated, may hold values from -4 to 4
- bins: int32 [64, 8], P(None, 'blk'), may hold values from 0 to 255
Outputs:
- record: float32 [64, 256], P('blk', 'tm')
Inputs may be any that keep to these rules, and one draw needn't show every extreme that they name: `dest`: each row names one source block; the rows of one partition name any block at most 24 times, and some partition names some block exactly 24 times.
All inputs are finite; a program needn't handle non-finite values.
Results may differ from a plain program's by a relative error of at most 0.0003.
Values may be sent and summed in bfloat16 or wider, within the bound.
No kernel may reach another device: no remote copies, remote signals or barrier semaphores. Data moves between devices by JAX's collectives and lax.ppermute only.
A program may use at most 128 MiB of HBM per device.

v0:
```python
import jax
import jax.numpy as jnp
from jax import lax
from jax.sharding import PartitionSpec as P


def stress_terms(density, flow_rest):
    rho = density.astype(jnp.float32)
    speed_x = flow_rest[..., 0, :, :].astype(jnp.float32)
    speed_y = flow_rest[..., 1, :, :].astype(jnp.float32)
    speed_z = flow_rest[..., 2, :, :].astype(jnp.float32)
    excess = flow_rest[..., 3, :, :].astype(jnp.float32)
    pieces = [
        rho * speed_x * speed_x + excess,
        rho * speed_y * speed_y + excess,
        rho * speed_z * speed_z + excess,
        rho * speed_x * speed_y,
        rho * speed_x * speed_z,
        rho * speed_y * speed_z,
    ]
    return jnp.stack(pieces, axis=-3)


def source_sums(grouped):
    return jnp.sum(grouped, axis=0)


def body(density, flow_rest, dest, weights, directions, bins):
    slab_len = density.shape[1]
    blocks = lax.axis_size("blk")
    targets = dest[:, 0]
    onehot = (targets[:, None] == jnp.arange(blocks, dtype=jnp.int32)[None, :]).astype(jnp.int32)
    stresses = stress_terms(density, flow_rest)
    membership = jnp.transpose(onehot).astype(jnp.float32)
    grouped = jnp.einsum("br,ritc->bitc", membership, stresses, precision=lax.Precision.HIGHEST)
    totals = source_sums(lax.all_to_all(grouped, "blk", split_axis=0, concat_axis=0, tiled=True))
    projector = jnp.stack(
        [
            directions[:, 0] * directions[:, 0],
            directions[:, 1] * directions[:, 1],
            directions[:, 2] * directions[:, 2],
            2.0 * directions[:, 0] * directions[:, 1],
            2.0 * directions[:, 0] * directions[:, 2],
            2.0 * directions[:, 1] * directions[:, 2],
        ],
        axis=1,
    )
    moment = jnp.einsum("oi,itc->otc", projector, totals, precision=lax.Precision.HIGHEST)
    source = jnp.sum(weights[0].astype(jnp.float32) * moment, axis=2)
    period = lax.all_gather(source, "tm", axis=1, tiled=True)
    steps_total = period.shape[1]
    curved = jnp.roll(period, -1, axis=1) - 2.0 * period + jnp.roll(period, 1, axis=1)
    out_times = lax.axis_index("tm") * slab_len + jnp.arange(slab_len, dtype=jnp.int32)
    lagged = jnp.mod(out_times[None, :] - bins, steps_total)
    shifted = jnp.take_along_axis(curved, lagged, axis=1)
    return lax.psum_scatter(shifted, "blk", scatter_dimension=0, tiled=True)


def solution(mesh):
    placed = (
        P("blk", "tm", None),
        P("blk", None, "tm", None),
        P("blk", None),
        P("blk", None, "tm", None),
        P(),
        P(None, "blk"),
    )
    return jax.shard_map(
        body, mesh=mesh, in_specs=placed, out_specs=P("blk", "tm"), check_vma=False
    )
```

profile of v0, /device:TPU:0, one launch (start us, length us, event | category | flops | bytes accessed | tf_op | source)
XLA Modules:
  0.0 152.6 jit_solution(10120597786458595526)
XLA Ops:
  0.0 0.0 copy-start
  0.0 4.5 %fusion.26 = (bf16[96,1,64,128]{3,2,1,0:T(8,128)(2,1)S(1)}, bf16[96,1,64,128]{3,2,1,0:T(8,128)(2,1)S(1)}, bf16[96,1,64,128]{3,2,1,0:T(8,128)(2,1)S(1)}, bf16[96,1,64,128]{3,2,1,0:T(8,128)(2,1)S(1)}) fusion(bf16[96,4,64,128]{3,2,1,0:T(8,128)(2,1)} %param.7), kind=kLoop, calls=%fused_computation.67 | loop fusion | bytes 12582912 | tf_op jit(solution)/shard_map/slice | solution.py:11
  4.5 0.0 copy-done
  4.5 2.5 %fusion.1 = f32[96,6,64,128]{3,0,2,1:T(8,128)S(1)} fusion(bf16[96,1,64,128]{3,2,1,0:T(8,128)(2,1)S(1)} %get-tuple-element.8, bf16[96,1,64,128]{3,2,1,0:T(8,128)(2,1)S(1)} %get-tuple-element.7, bf16[96,64,128]{2,1,0:T(8,128)(2,1)S(1)} %copy-done), kind=kLoop, calls=%fused_computation.14 | loop fusion | flops 4718591 | bytes 7864320
  7.0 2.5 %fusion.3 = f32[96,6,64,128]{3,0,2,1:T(8,128)S(1)} fusion(f32[96,6,64,128]{3,0,2,1:T(8,128)S(1)} %fusion.1, bf16[96,1,64,128]{3,2,1,0:T(8,128)(2,1)S(1)} %get-tuple-element.7, bf16[96,1,64,128]{3,2,1,0:T(8,128)(2,1)S(1)} %get-tuple-element.6, bf16[96,64,128]{2,1,0:T(8,128)(2,1)S(1)} %copy-done), kind=kLoop, calls=%fused_computation.16 | loop fusion | flops 4718592 | bytes 7864320
  9.6 2.5 %fusion.5 = f32[96,6,64,128]{3,0,2,1:T(8,128)S(1)} fusion(f32[96,6,64,128]{3,0,2,1:T(8,128)S(1)} %fusion.3, bf16[96,1,64,128]{3,2,1,0:T(8,128)(2,1)S(1)} %get-tuple-element.7, bf16[96,1,64,128]{3,2,1,0:T(8,128)(2,1)S(1)} %get-tuple-element.5, bf16[96,64,128]{2,1,0:T(8,128)(2,1)S(1)} %copy-done), kind=kLoop, calls=%fused_computation.18 | loop fusion | flops 4718592 | bytes 7864320
  12.1 2.7 %fusion.7 = f32[96,6,64,128]{3,0,2,1:T(8,128)S(1)} fusion(f32[96,6,64,128]{3,0,2,1:T(8,128)S(1)} %fusion.5, bf16[96,1,64,128]{3,2,1,0:T(8,128)(2,1)S(1)} %get-tuple-element.8, bf16[96,1,64,128]{3,2,1,0:T(8,128)(2,1)S(1)} %get-tuple-element.6, bf16[96,64,128]{2,1,0:T(8,128)(2,1)S(1)} %copy-done), kind=kLoop, calls=%fused_computation.20 | loop fusion | flops 3932160 | bytes 7864320
  14.8 2.5 %fusion.9 = f32[96,6,64,128]{3,0,2,1:T(8,128)S(1)} fusion(f32[96,6,64,128]{3,0,2,1:T(8,128)S(1)} %fusion.7, bf16[96,1,64,128]{3,2,1,0:T(8,128)(2,1)S(1)} %get-tuple-element.8, bf16[96,1,64,128]{3,2,1,0:T(8,128)(2,1)S(1)} %get-tuple-element.5, bf16[96,64,128]{2,1,0:T(8,128)(2,1)S(1)} %copy-done), kind=kLoop, calls=%fused_computation.22 | loop fusion | flops 3932160 | bytes 7864320
  17.4 0.0 copy-start.3
  17.4 2.5 %fusion.11 = f32[96,6,64,128]{3,0,2,1:T(8,128)S(1)} fusion(f32[96,6,64,128]{3,0,2,1:T(8,128)S(1)} %fusion.9, bf16[96,1,64,128]{3,2,1,0:T(8,128)(2,1)S(1)} %get-tuple-element.6, bf16[96,1,64,128]{3,2,1,0:T(8,128)(2,1)S(1)} %get-tuple-element.5, bf16[96,64,128]{2,1,0:T(8,128)(2,1)S(1)} %copy-done), kind=kLoop, calls=%fused_computation.24 | loop fusion | flops 3932160 | bytes 7864320 | tf_op jit(solution)/shard_map/stack | solution.py:21
  19.9 0.0 copy-done.3
  19.9 9.2 %fusion.20 = f32[8,6,64,128]{3,0,2,1:T(8,128)S(1)} fusion(f32[96,6,64,128]{3,0,2,1:T(8,128)S(1)} %fusion.11, s32[96]{0:T(128)S(1)} %bitcast.79), kind=kOutput, calls=%fused_computation.52 | convolution fusion | flops 452987136 | bytes 20447616 | tf_op jit(solution)/shard_map/br,ritc->bitc/dot_general | solution.py:35
  29.2 1.5 copy.32
  30.6 0.0 copy-start.1
  30.6 0.0 copy-start.5
  30.6 0.0 copy-start.2
  30.6 0.0 copy-start.4
  30.6 7.4 %all-to-all-start = ((f32[8,6,64,128]{3,2,1,0:T(8,128)}), f32[8,6,64,128]{3,2,1,0:T(8,128)S(1)}, u32[]{:S(2)}, u32[]{:S(2)}) async-start(f32[8,6,64,128]{3,2,1,0:T(8,128)} %copy.32), calls=%async_computation | async-start | bytes 3145728 | tf_op jit(solution)/shard_map/all_to_all | solution.py:36
  38.0 0.0 copy-done.1
  38.1 0.1 fusion.19
  38.2 0.1 reshape.129
  38.2 0.0 copy-done.5
  38.2 0.6 dynamic-slice
  39.5 0.0 copy-done.2
  39.5 35.5 %all-to-all-done = f32[8,6,64,128]{3,2,1,0:T(8,128)S(1)} async-done(((f32[8,6,64,128]{3,2,1,0:T(8,128)}), f32[8,6,64,128]{3,2,1,0:T(8,128)S(1)}, u32[]{:S(2)}, u32[]{:S(2)}) %all-to-all-start) | async-done | bytes 1572896 | tf_op jit(solution)/shard_map/all_to_all | solution.py:36
  75.0 0.1 reduce_sum.18
  75.1 0.0 copy-done.4
  75.1 2.8 %fusion.12 = f32[64,64]{0,1:T(8,128)S(1)} fusion(bf16[1,64,64,128]{3,2,1,0:T(8,128)(2,1)S(1)} %copy-done.4, f32[6,64,128]{2,1,0:T(8,128)S(1)} %reduce_sum.18, f32[64,6]{0,1:T(8,128)S(1)} %stack.30), kind=kOutput, calls=%fused_computation.26 | convolution fusion | flops 39317504 | bytes 1263104 | tf_op jit(solution)/shard_map/oi,itc->otc/dot_general | solution.py:48
  77.9 5.4 %all_gather.3 = f32[64,256]{0,1:T(8,128)S(1)} all-gather(f32[64,64]{0,1:T(8,128)S(1)} %fusion.12), channel_id=1, replica_groups=mesh['blk'=8,'tm'=4] {'tm'}, dimensions={1}, use_global_device_ids=true | all-gather | bytes 81920 | tf_op jit(solution)/shard_map/all_gather | solution.py:50
  83.4 0.1 copy.35
  83.5 0.1 fusion.28
  83.5 0.1 copy.36
  83.6 0.1 copy.39
  83.7 0.1 fusion.14
  83.8 32.8 %gather_fusion = f32[4096]{0:T(1024)S(1)} fusion(f32[64,256]{1,0:T(8,128)S(1)} %fusion.14, s32[4096]{0:T(1024)S(1)} %reshape.129), kind=kCustom, calls=%fused_computation | custom fusion | bytes 65536 | tf_op jit(solution)/shard_map/jit(take_along_axis)/gather | solution.py:55
  116.6 0.1 reshape.132
  116.7 0.1 and_select_fusion
  116.8 35.2 %all-reduce = f32[64,64]{1,0:T(8,128)S(1)} all-reduce(f32[64,64]{1,0:T(8,128)S(1)} %and_select_fusion), channel_id=2, replica_groups=mesh['blk'=8,'tm'=4] {'blk'}, use_global_device_ids=true, to_apply=%region_2.3.clone | all-reduce | flops 4096 | bytes 32768
  152.0 0.6 constant_dynamic-slice_fusion
  (4 shorter events, 0.0 us)
Async XLA Ops:
  0.0 4.5 %copy-start = (bf16[96,64,128]{2,1,0:T(8,128)(2,1)S(1)}, bf16[96,64,128]{2,1,0:T(8,128)(2,1)}, u32[]{:S(2)}) copy-start(bf16[96,64,128]{2,1,0:T(8,128)(2,1)} %param.6) | copy-start | bytes 4718596
  17.4 2.6 %copy-start.3 = (s32[96,1]{0,1:T(1,128)S(1)}, s32[96,1]{0,1:T(1,128)}, u32[]{:S(2)}) copy-start(s32[96,1]{0,1:T(1,128)} %param.8) | copy-start | bytes 1156
  30.6 7.4 %copy-start.1 = (s32[64,1]{0,1:T(1,128)S(1)}, s32[64,1]{0,1:T(1,128)}, u32[]{:S(2)}) copy-start(s32[64,1]{0,1:T(1,128)} %param.11) | copy-start | bytes 772
  30.6 7.6 %copy-start.5 = (u32[32]{0:T(128)S(1)}, u32[32]{0:T(128)}, u32[]{:S(2)}) copy-start(u32[32]{0:T(128)} %constant.58) | copy-start | bytes 388
  30.6 8.8 %copy-start.2 = (f32[64,3]{0,1:T(4,128)S(1)}, f32[64,3]{0,1:T(4,128)}, u32[]{:S(2)}) copy-start(f32[64,3]{0,1:T(4,128)} %param.10) | copy-start | bytes 2308
  30.6 44.5 %copy-start.4 = (bf16[1,64,64,128]{3,2,1,0:T(8,128)(2,1)S(1)}, bf16[1,64,64,128]{3,2,1,0:T(8,128)(2,1)}, u32[]{:S(2)}) copy-start(bf16[1,64,64,128]{3,2,1,0:T(8,128)(2,1)} %param.9) | copy-start | bytes 3145732
  30.6 44.4 %all-to-all-start = ((f32[8,6,64,128]{3,2,1,0:T(8,128)}), f32[8,6,64,128]{3,2,1,0:T(8,128)S(1)}, u32[]{:S(2)}, u32[]{:S(2)}) async-start(f32[8,6,64,128]{3,2,1,0:T(8,128)} %copy.32), calls=%async_computation | async-start | bytes 3145728 | tf_op jit(solution)/shard_map/all_to_all | solution.py:36
where the time goes:
time: 153 us
  blocking collectives  40.6 us (27%)
  local copies, waits for them, and re-layouts  40.4 us (26%)
  waiting for transfers between devices  35.5 us (23%)
  other arithmetic  15.8 us (10%)
  matrix products  12 us (8%)
  starting transfers between devices  7.4 us (5%)
    all_to_all x1, waiting for transfers between devices, body(): lax.all_to_all(grouped, 'blk', split_axis=0, concat_axis=0, tiled=True)  35.5 us
    unnamed x1, blocking collectives  35.2 us
    gather x3, local copies, waits for them, and re-layouts, body(): shifted = jnp.take_along_axis(curved, lagged, axis=1)  32.9 us
    unnamed x5, other arithmetic  12.9 us
    dot_general x1, matrix products, body(): jnp.einsum('br,ritc->bitc', membership, stresses, precision=lax.Precision...  9.23 us
    all_to_all x1, starting transfers between devices, body(): lax.all_to_all(grouped, 'blk', split_axis=0, concat_axis=0, tiled=True)  7.4 us
    all_gather x1, blocking collectives, body(): period = lax.all_gather(source, 'tm', axis=1, tiled=True)  5.43 us
    slice x1, local copies, waits for them, and re-layouts, stress_terms(): speed_z = flow_rest[..., 2, :, :].astype(jnp.float32)  4.47 us
  transfers between devices with their start and end apart: 1, of which 1 were waited for; matrix products, arithmetic and copies ran while one was open for 1% of the time, Pallas kernels for 0%

commit v1 on v0

v1 whole, which is shorter than its diff:
```python
import functools

import jax
import jax.numpy as jnp
from jax import lax
from jax.experimental import pallas as pl
from jax.experimental.pallas import tpu as pltpu
from jax.sharding import PartitionSpec as P

COMPS = 6
TILE = 16
LANES = 128
UNROLL = 4
GRAIN = 128.0
TOP = 32764.0
FLOOR = 1e-35
VMEM_BYTES = 48 * 1024 * 1024


def whole():
    return pl.BlockSpec(memory_space=pltpu.VMEM)


def scalars():
    return pl.BlockSpec(memory_space=pltpu.SMEM)


def params():
    return pltpu.CompilerParams(vmem_limit_bytes=VMEM_BYTES)


def scale_code(largest):
    return jnp.ceil(jnp.log(jnp.maximum(largest, FLOOR)) * GRAIN)


def encode(values, inverse):
    return jnp.round(values * inverse).astype(jnp.int32).astype(jnp.int16)


def encode_factor(code):
    return jnp.exp(code * (-1.0 / GRAIN)) * TOP


def decode_factor(code16):
    code = code16.astype(jnp.int32).astype(jnp.float32)
    return jnp.exp(code * (1.0 / GRAIN)) * (1.0 / TOP)


def decode(code16, factor):
    return code16.astype(jnp.int32).astype(jnp.float32) * factor


def with_bit(index, position, bit):
    low = index & ((1 << position) - 1)
    return ((index >> position) << (position + 1)) | (bit << position) | low


def rows_at(start, size=TILE):
    return pl.ds(pl.multiple_of(start, TILE), size)


def write_codes(largest, staged, send_ref, rows):
    code = scale_code(largest)
    inverse = encode_factor(code)

    def step(k, carry):
        where = rows_at(k * TILE)
        send_ref[where, :] = encode(staged[where, :], inverse)
        return carry

    lax.fori_loop(0, rows // TILE, step, 0, unroll=4)
    send_ref[rows:rows + TILE, :] = code.astype(jnp.int32).astype(jnp.int16)


def stress_kernel(blocks, bits, dest_ref, density_ref, flow_ref, *refs):
    halves = len(bits)
    sends, keeps = refs[:halves], refs[halves:2 * halves]
    dens, flow, staged, counts, members, sems = refs[2 * halves:]
    rows, steps = density_ref.shape[0], density_ref.shape[1]
    tiles = steps // TILE
    per_half = tiles // halves
    span = steps // halves
    copies = []
    for k in range(tiles):
        at = pl.ds(k * TILE, TILE)
        copies.append((
            pltpu.make_async_copy(density_ref.at[:, at, :], dens.at[pl.ds(0, rows), at, :], sems.at[k, 0]),
            pltpu.make_async_copy(flow_ref.at[:, :, at, :], flow.at[pl.ds(0, rows), :, at, :], sems.at[k, 1]),
        ))
    for pair in copies:
        for copy in pair:
            copy.start()

    dens[rows] = jnp.zeros_like(dens[rows])
    flow[rows] = jnp.zeros_like(flow[rows])
    stride = rows + UNROLL

    def clear(b, carry):
        counts[b] = 0
        return carry

    lax.fori_loop(0, blocks, clear, 0)

    def place(r, carry):
        target = dest_ref[r]
        count = counts[target]
        members[target * stride + count] = r
        counts[target] = count + 1
        return carry

    lax.fori_loop(0, rows, place, 0, unroll=4)

    def pad(b, carry):
        end = b * stride + counts[b]
        for extra in range(UNROLL - 1):
            members[end + extra] = rows
        return carry

    lax.fori_loop(0, blocks, pad, 0)

    me = lax.axis_index("blk")

    def sums(slot, at):
        target = me ^ slot
        first = target * stride

        def body(turn, totals):
            totals = list(totals)
            for u in range(UNROLL):
                row = members[first + turn * UNROLL + u]
                rho = dens[row, at, :].astype(jnp.float32)
                ux = flow[row, 0, at, :].astype(jnp.float32)
                uy = flow[row, 1, at, :].astype(jnp.float32)
                uz = flow[row, 2, at, :].astype(jnp.float32)
                excess = flow[row, 3, at, :].astype(jnp.float32)
                mx, my, mz = rho * ux, rho * uy, rho * uz
                for i, term in enumerate((mx * ux, my * uy, mz * uz, mx * uy, mx * uz, my * uz, excess)):
                    totals[i] = totals[i] + term
            return tuple(totals)

        zero = jnp.zeros((TILE, LANES), jnp.float32)
        turns = (counts[target] + (UNROLL - 1)) // UNROLL
        xx, yy, zz, xy, xz, yz, excess = lax.fori_loop(0, turns, body, (zero,) * 7)
        return xx + excess, yy + excess, zz + excess, xy, xz, yz

    for half in range(halves):
        largest = jnp.zeros((TILE, LANES), jnp.float32)
        for k in range(per_half):
            tile = half * per_half + k
            at = slice(tile * TILE, (tile + 1) * TILE)
            for copy in copies[tile]:
                copy.wait()

            def sent(i, top):
                pieces = sums(with_bit(i, bits[half], 1), at)
                for c, piece in enumerate(pieces):
                    staged[rows_at((i * COMPS + c) * span + k * TILE), :] = piece
                    top = jnp.maximum(top, jnp.abs(piece))
                return top

            largest = lax.fori_loop(0, blocks // 2, sent, largest)

            def kept(i, carry):
                pieces = sums(with_bit(i, bits[half], 0), at)
                for c, piece in enumerate(pieces):
                    keeps[half][rows_at((i * COMPS + c) * span + k * TILE), :] = piece
                return carry

            lax.fori_loop(0, blocks // 2, kept, 0)
        write_codes(largest, staged, sends[half], blocks // 2 * COMPS * span)


def stress_sums(density, flow_rest, targets, blocks, bits):
    rows, steps, _ = density.shape
    halves = len(bits)
    sent = blocks // 2 * COMPS * (steps // halves)
    outs = [jax.ShapeDtypeStruct((sent + TILE, LANES), jnp.int16)] * halves
    outs += [jax.ShapeDtypeStruct((sent, LANES), jnp.float32)] * halves
    got = pl.pallas_call(
        functools.partial(stress_kernel, blocks, bits),
        out_shape=outs,
        in_specs=[scalars(), pl.BlockSpec(memory_space=pl.ANY), pl.BlockSpec(memory_space=pl.ANY)],
        out_specs=[whole()] * len(outs),
        scratch_shapes=[
            pltpu.VMEM((rows + 1, steps, LANES), density.dtype),
            pltpu.VMEM((rows + 1, flow_rest.shape[1], steps, LANES), flow_rest.dtype),
            pltpu.VMEM((sent, LANES), jnp.float32),
            pltpu.SMEM((blocks,), jnp.int32),
            pltpu.SMEM((blocks * (rows + UNROLL),), jnp.int32),
            pltpu.SemaphoreType.DMA((steps // TILE, 2)),
        ],
        compiler_params=params(),
        name="stress_sums",
    )(targets, density, flow_rest)
    return got[:halves], got[halves:]


def merge_kernel(count, position, block_rows, joined, *refs):
    pieces = len(block_rows)
    groups = 1 if joined else pieces
    got, kept = refs[:pieces], refs[pieces:2 * pieces]
    sends, keeps = refs[2 * pieces:2 * pieces + groups], refs[2 * pieces + groups:2 * pieces + 2 * groups]
    staged = refs[-1]
    half = count // 2
    largest = jnp.zeros((TILE, LANES), jnp.float32)
    for p in range(pieces):
        size = block_rows[p]
        group = 0 if joined else p
        pitch = sum(block_rows) if joined else size
        offset = sum(block_rows[:p]) if joined else 0
        factor = decode_factor(got[p][count * size:count * size + TILE, :])
        if not joined:
            largest = jnp.zeros((TILE, LANES), jnp.float32)

        def total(block, k):
            where = rows_at(block * size + k * TILE)
            return kept[p][where, :] + decode(got[p][where, :], factor)

        def sent(i, top):
            def tile(k, top):
                piece = total(with_bit(i, position[p], 1), k)
                staged[rows_at(i * pitch + offset + k * TILE), :] = piece
                return jnp.maximum(top, jnp.abs(piece))

            return lax.fori_loop(0, size // TILE, tile, top, unroll=4)

        largest = lax.fori_loop(0, half, sent, largest)

        def stay(i, carry):
            def tile(k, carry):
                keeps[group][rows_at(i * pitch + offset + k * TILE), :] = total(with_bit(i, position[p], 0), k)
                return carry

            return lax.fori_loop(0, size // TILE, tile, carry, unroll=4)

        lax.fori_loop(0, half, stay, 0)
        if not joined or p == pieces - 1:
            write_codes(largest, staged, sends[group], half * pitch)


def merge(got, kept, count, position, block_rows, joined):
    half = count // 2
    pitches = [sum(block_rows)] if joined else list(block_rows)
    outs = [jax.ShapeDtypeStruct((half * pitch + TILE, LANES), jnp.int16) for pitch in pitches]
    outs += [jax.ShapeDtypeStruct((half * pitch, LANES), jnp.float32) for pitch in pitches]
    made = pl.pallas_call(
        functools.partial(merge_kernel, count, tuple(position), tuple(block_rows), joined),
        out_shape=outs,
        in_specs=[whole()] * (2 * len(got)),
        out_specs=[whole()] * len(outs),
        scratch_shapes=[pltpu.VMEM((half * max(pitches), LANES), jnp.float32)],
        compiler_params=params(),
        name="merge",
    )(*got, *kept)
    return made[:len(pitches)], made[len(pitches):]


def source_kernel(halves, per_device, copies, proj_ref, got_ref, kept_ref, weights_ref, out_ref, totals, source):
    observers, steps, _ = weights_ref.shape
    span = steps // halves
    factor = decode_factor(got_ref[COMPS * steps:COMPS * steps + TILE, :])

    def fill(k, carry):
        where = rows_at(k * TILE)
        totals[where, :] = kept_ref[where, :] + decode(got_ref[where, :], factor)
        return carry

    lax.fori_loop(0, COMPS * steps // TILE, fill, 0, unroll=4)
    lane = lax.broadcasted_iota(jnp.int32, (TILE, LANES), 1)

    def times(tile, carry):
        half = tile // (span // TILE)
        inside = tile - half * (span // TILE)
        parts = [totals[rows_at((half * COMPS + c) * span + inside * TILE), :] for c in range(COMPS)]

        def weighted(o):
            moment = proj_ref[o * COMPS] * parts[0]
            for c in range(1, COMPS):
                moment = moment + proj_ref[o * COMPS + c] * parts[c]
            return weights_ref[o, rows_at(tile * TILE), :].astype(jnp.float32) * moment

        def summed(first, number):
            if number == 1:
                return weighted(first)
            step = number // 2
            return join(first, number, step)

        def join(first, number, step):
            even = summed_at(first, number, 0)
            odd = summed_at(first, number, step)
            clear = (lane & step) == 0
            return jnp.where(clear, even, odd) + pltpu.roll(jnp.where(clear, odd, even), step, 1)

        def summed_at(first, number, extra):
            return summed(first + extra, number // 2)

        value = summed(0, observers)
        width = observers
        while width < LANES:
            value = value + pltpu.roll(value, width, 1)
            width *= 2
        source[rows_at(tile * TILE), :] = value
        source[rows_at(steps + tile * TILE), :] = value
        return carry

    lax.fori_loop(0, steps // TILE, times, 0)
    across = source[...].T
    if per_device % 2 == 0:
        half = per_device // 2
        lanes = lax.broadcasted_iota(jnp.int32, (per_device, LANES), 1)
        for b in range(observers // per_device):
            mine = across[b * per_device:(b + 1) * per_device]
            packed = jnp.where(lanes < steps, mine, jnp.concatenate([mine[half:], mine[:half]], axis=0))[:half]
            for copy in range(copies):
                out_ref[b * copies + copy] = packed
    else:
        for b in range(observers // per_device):
            for copy in range(copies):
                out_ref[b * copies + copy] = across[b * per_device:(b + 1) * per_device]


def sources(projector, got, kept, weights, halves, blocks, copies):
    observers, steps, _ = weights.shape
    per_device = observers // blocks
    rows = per_device // 2 if per_device % 2 == 0 else per_device
    return pl.pallas_call(
        functools.partial(source_kernel, halves, per_device, copies),
        out_shape=jax.ShapeDtypeStruct((blocks * copies, rows, LANES), jnp.float32),
        in_specs=[scalars()] + [whole()] * 3,
        out_specs=whole(),
        scratch_shapes=[
            pltpu.VMEM((COMPS * steps, LANES), jnp.float32),
            pltpu.VMEM((2 * steps, LANES), jnp.float32),
        ],
        compiler_params=params(),
        name="sources",
    )(projector, got, kept, weights)


def record_kernel(blocks, slabs, steps, got_ref, delay_ref, out_ref):
    per_device = out_ref.shape[0]
    period = slabs * steps
    lanes = lax.broadcasted_iota(jnp.int32, (per_device, LANES), 1)
    row = lax.broadcasted_iota(jnp.int32, (per_device, LANES), 0)
    packed = per_device % 2 == 0

    def unpacked(chunk):
        if not packed:
            return chunk, chunk
        both = jnp.concatenate([chunk, chunk], axis=0)
        turned = pltpu.roll(both, steps, 1)
        upper = row < per_device // 2
        return jnp.where(upper, both, turned), jnp.where(upper, turned, both)

    pieces, delays = [], []
    for b in range(blocks):
        columns = []
        for s in range(0, slabs, 2):
            low, _ = unpacked(got_ref[b * slabs + s])
            _, high = unpacked(got_ref[b * slabs + s + 1])
            columns.append(jnp.where(lanes < steps, low, high))
        pieces.append(jnp.concatenate(columns, axis=1))
        delays.append(delay_ref[b * slabs])
    value = jnp.concatenate(pieces, axis=0)
    delay = jnp.concatenate(delays, axis=0)
    delay = delay - lax.axis_index("tm") * steps
    delay = jnp.where(delay < 0, delay + period, delay)
    delay = jnp.concatenate([delay] * (period // LANES), axis=1)
    shift = 1
    while shift < period:
        value = jnp.where((delay & shift) != 0, pltpu.roll(value, shift, 1), value)
        shift *= 2
    total = value[:per_device]
    for b in range(1, blocks):
        total = total + value[b * per_device:(b + 1) * per_device]
    curved = pltpu.roll(total, period - 1, 1) - 2.0 * total + pltpu.roll(total, 1, 1)
    out_ref[...] = curved[:, :steps]


def records(got, delays, blocks, slabs, steps, per_device):
    return pl.pallas_call(
        functools.partial(record_kernel, blocks, slabs, steps),
        out_shape=jax.ShapeDtypeStruct((per_device, steps), jnp.float32),
        in_specs=[whole()] * 2,
        out_specs=whole(),
        compiler_params=params(),
        name="records",
    )(got, delays)


def body(density, flow_rest, dest, weights, directions, bins):
    blocks, slabs = lax.axis_size("blk"), lax.axis_size("tm")
    steps = density.shape[1]
    observers = bins.shape[0]
    per_device = observers // blocks

    def swap(values, bit):
        return lax.ppermute(values, "blk", [(i, i ^ (1 << bit)) for i in range(blocks)])

    orders = ((0, 1), (1, 0))
    (send_a, send_b), (keep_a, keep_b) = stress_sums(
        density, flow_rest, dest[:, 0], blocks, tuple(order[0] for order in orders)
    )
    span_rows = COMPS * (steps // 2)
    got = [swap(send_a, 0), swap(send_b, 1)]

    delays = jnp.broadcast_to(
        bins.reshape(blocks, 1, per_device, 1), (blocks, slabs, per_device, LANES)
    ).reshape(blocks * slabs, per_device, LANES)
    delays = lax.all_to_all(delays, ("blk", "tm"), split_axis=0, concat_axis=0, tiled=True)

    count = blocks // 2
    (send_a, send_b), (keep_a, keep_b) = merge(
        got, [keep_a, keep_b], count, [0, 0], [span_rows, span_rows], False
    )
    got = [swap(send_a, 1), swap(send_b, 0)]
    count //= 2
    kept, sizes, joined, bit = [keep_a, keep_b], [span_rows, span_rows], True, 2
    while count > 1:
        (send,), (keep,) = merge(got, kept, count, [0] * len(got), sizes, joined)
        got, kept, sizes = [swap(send, bit)], [keep], [2 * span_rows]
        count //= 2
        bit += 1

    d1, d2, d3 = directions[:, 0], directions[:, 1], directions[:, 2]
    projector = jnp.stack(
        [d1 * d1, d2 * d2, d3 * d3, 2.0 * d1 * d2, 2.0 * d1 * d3, 2.0 * d2 * d3], axis=1
    ).reshape(observers * COMPS)
    chunks = sources(projector, got[0], kept[0], weights[0], 2, blocks, slabs)
    chunks = lax.all_to_all(chunks, ("blk", "tm"), split_axis=0, concat_axis=0, tiled=True)
    return records(chunks, delays, blocks, slabs, steps, per_device)


def solution(mesh):
    placed = (
        P("blk", "tm", None),
        P("blk", None, "tm", None),
        P("blk", None),
        P("blk", None, "tm", None),
        P(),
        P(None, "blk"),
    )
    return jax.shard_map(
        body, mesh=mesh, in_specs=placed, out_specs=P("blk", "tm"), check_vma=False
    )
```

time: 153 us -> 54.7 us (0.36)
  local copies, waits for them, and re-layouts: 40.4 us -> 3.7 us
  blocking collectives: 40.6 us -> 10.8 us
  waiting for transfers between devices: 35.5 us -> 12.7 us
  other arithmetic: 15.8 us -> 0.67 us
  Pallas kernels: 0 us -> 12.1 us
  matrix products: 12 us -> 0 us
  starting transfers between devices: 7.4 us -> 14.5 us
    all_to_all x1, waiting for transfers between devices: 35.5 us -> 0.01 us  [body(): lax.all_to_all(delays, ('blk', 'tm'), split_axis=0, concat_axis=0, tiled=...]
    unnamed x1 -> x0, blocking collectives: 35.2 us -> none
    gather x3 -> x0, local copies, waits for them, and re-layouts: 32.9 us -> none  [body(): shifted = jnp.take_along_axis(curved, lagged, axis=1)]
    ppermute x0 -> x5, waiting for transfers between devices: none -> 12.7 us  [swap(): lax.ppermute(values, 'blk', [(i, i ^ 1 << bit) for i in range(blocks)])]
    unnamed x5 -> x1, other arithmetic: 12.9 us -> 0.66 us
    pallas_call x0 -> x5, Pallas kernels: none -> 12.1 us  [the longest x1 6.26 us: stress_sums(): pl.pallas_call(functools.partial(stress_kernel, blocks, bits), out_shape=...]
    dot_general x2 -> x0, matrix products: 12 us -> none  [the longest x1 9.23 us: body(): jnp.einsum('br,ritc->bitc', membership, stresses, precision=lax.Precision...]
    all_to_all x0 -> x1, blocking collectives: none -> 10.8 us  [body(): lax.all_to_all(chunks, ('blk', 'tm'), split_axis=0, concat_axis=0, tiled=...]
  transfers between devices with their start and end apart: 1 -> 6, of which waited for: 1 -> 3; matrix products, arithmetic and copies ran while one was open for 1% -> 4% of each run, Pallas kernels for 0% -> 7%
where the time goes in v1:
time: 54.7 us; the launch traced here: 54.5 us
  starting transfers between devices  14.5 us (27%)
  waiting for transfers between devices  12.7 us (23%)
  Pallas kernels  12.1 us (22%)
  blocking collectives  10.8 us (20%)
  local copies, waits for them, and re-layouts  3.7 us (7%)
  other arithmetic  0.67 us (1%)
    ppermute x5, waiting for transfers between devices, swap(): lax.ppermute(values, 'blk', [(i, i ^ 1 << bit) for i in range(blocks)])  12.7 us
    all_to_all x1, blocking collectives, body(): lax.all_to_all(chunks, ('blk', 'tm'), split_axis=0, concat_axis=0, tiled=...  10.8 us
    ppermute x5, starting transfers between devices, swap(): lax.ppermute(values, 'blk', [(i, i ^ 1 << bit) for i in range(blocks)])  9.5 us
    pallas_call x1, Pallas kernels, stress_sums(): pl.pallas_call(functools.partial(stress_kernel, blocks, bits), out_shape=...  6.26 us
    all_to_all x1, starting transfers between devices, body(): lax.all_to_all(delays, ('blk', 'tm'), split_axis=0, concat_axis=0, tiled=...  4.96 us
    pallas_call x1, Pallas kernels, sources(): pl.pallas_call(functools.partial(source_kernel, halves, per_device, copie...  3.82 us
    unnamed x11, local copies, waits for them, and re-layouts  2.6 us
    pallas_call x1, Pallas kernels, records(): pl.pallas_call(functools.partial(record_kernel, blocks, slabs, steps), ou...  1.25 us
  transfers between devices with their start and end apart: 6, of which 3 were waited for; matrix products, arithmetic and copies ran while one was open for 4% of the time, Pallas kernels for 7%

profile of v1, /device:TPU:0, one launch (start us, length us, event | category | flops | bytes accessed | tf_op | source)
XLA Modules:
  0.0 54.5 jit_solution(8663977286818146042)
XLA Ops:
  0.0 0.0 copy-start.4
  0.0 0.0 copy-start
  0.0 1.4 %copy-done = bf16[96,64,128]{2,1,0:T(8,128)(2,1)S(1)} copy-done((bf16[96,64,128]{2,1,0:T(8,128)(2,1)S(1)}, bf16[96,64,128]{2,1,0:T(8,128)(2,1)}, u32[]{:S(2)}) %copy-start) | copy-done | bytes 1572888
  1.4 0.0 copy-start.2
  1.4 0.7 %copy-done.2 = s32[96,1]{0,1:T(1,128)S(1)} copy-done((s32[96,1]{0,1:T(1,128)S(1)}, s32[96,1]{0,1:T(1,128)}, u32[]{:S(2)}) %copy-start.2) | copy-done | bytes 408
  2.1 0.0 copy-start.3
  2.1 0.0 copy-start.1
  2.1 6.3 %stress_sums.1 = (s16[784,128]{1,0:T(8,128)(2,1)S(1)}, s16[784,128]{1,0:T(8,128)(2,1)S(1)}, f32[768,128]{1,0:T(8,128)S(1)}, f32[768,128]{1,0:T(8,128)S(1)}) custom-call(s32[96]{0:T(128)S(1)} %bitcast.5, bf16[96,64,128]{2,1,0:T(8,128)(2,1)S(1)} %copy-done, bf16[96,4,64,128]{3,2,1,0:T(8,128)(2,1)} %flow_ref.1), custom_call_target="tpu_custom_call" | custom-call | tf_op jit(solution)/shard_map/stress_sums/pallas_call | solution.py:179
  8.4 3.1 %collective-permute-start = (s16[784,128]{1,0:T(8,128)(2,1)S(1)}, s16[784,128]{1,0:T(8,128)(2,1)S(1)}, u32[]{:S(2)}, u32[]{:S(2)}) collective-permute-start(s16[784,128]{1,0:T(8,128)(2,1)S(1)} %get-tuple-element.15), channel_id=1, source_target_pairs={{0,4},{4,0},{8,12},{12,8},{16,20},{20,16},{24,28},{28,24},{1,5},{5... | collective-permute-start | bytes 602120 | tf_op jit(solution)/shard_map/ppermute | solution.py:398
  11.5 1.5 %collective-permute-start.1 = (s16[784,128]{1,0:T(8,128)(2,1)S(1)}, s16[784,128]{1,0:T(8,128)(2,1)S(1)}, u32[]{:S(2)}, u32[]{:S(2)}) collective-permute-start(s16[784,128]{1,0:T(8,128)(2,1)S(1)} %get-tuple-element.16), channel_id=1, source_target_pairs={{0,8},{4,12},{8,0},{12,4},{16,24},{20,28},{24,16},{28,20},{1,9},{5... | collective-permute-start | bytes 602120 | tf_op jit(solution)/shard_map/ppermute | solution.py:398
  12.9 3.5 %collective-permute-done.refs_0_ = s16[784,128]{1,0:T(8,128)(2,1)S(1)} collective-permute-done((s16[784,128]{1,0:T(8,128)(2,1)S(1)}, s16[784,128]{1,0:T(8,128)(2,1)S(1)}, u32[]{:S(2)}, u32[]{:S(2)}) %collective-permute-start) | collective-permute-done | bytes 200736 | tf_op jit(solution)/shard_map/ppermute | solution.py:398
  16.5 1.5 %collective-permute-done.1.refs_1_ = s16[784,128]{1,0:T(8,128)(2,1)S(1)} collective-permute-done((s16[784,128]{1,0:T(8,128)(2,1)S(1)}, s16[784,128]{1,0:T(8,128)(2,1)S(1)}, u32[]{:S(2)}, u32[]{:S(2)}) %collective-permute-start.1) | collective-permute-done | bytes 200736 | tf_op jit(solution)/shard_map/ppermute | solution.py:398
  17.9 0.5 merge.2
  18.5 1.5 %collective-permute-start.2 = (s16[400,128]{1,0:T(8,128)(2,1)S(1)}, s16[400,128]{1,0:T(8,128)(2,1)S(1)}, u32[]{:S(2)}, u32[]{:S(2)}) collective-permute-start(s16[400,128]{1,0:T(8,128)(2,1)S(1)} %get-tuple-element.19), channel_id=1, source_target_pairs={{0,8},{4,12},{8,0},{12,4},{16,24},{20,28},{24,16},{28,20},{1,9},{5... | collective-permute-start | bytes 307208 | tf_op jit(solution)/shard_map/ppermute | solution.py:398
  20.0 0.7 %collective-permute-start.3 = (s16[400,128]{1,0:T(8,128)(2,1)S(1)}, s16[400,128]{1,0:T(8,128)(2,1)S(1)}, u32[]{:S(2)}, u32[]{:S(2)}) collective-permute-start(s16[400,128]{1,0:T(8,128)(2,1)S(1)} %get-tuple-element.20), channel_id=1, source_target_pairs={{0,4},{4,0},{8,12},{12,8},{16,20},{20,16},{24,28},{28,24},{1,5},{5... | collective-permute-start | bytes 307208 | tf_op jit(solution)/shard_map/ppermute | solution.py:398
  20.6 0.5 broadcast.15
  21.1 0.0 copy-done.4
  21.2 0.7 %reduce.3 = s32[64]{0:T(128)S(1)} reduce(s32[64,1]{0,1:T(1,128)S(1)} %copy-done.4, s32[]{:T(128)} %broadcast.15), dimensions={1}, to_apply=%param.11.reduce_sub_computation.3 | reduce | bytes 516 | tf_op args[5]
  21.8 0.1 broadcast_in_dim.11
  21.9 0.8 %broadcast_in_dim.14 = s32[32,8,128]{2,1,0:T(8,128)} broadcast(s32[32,8]{1,0:T(8,128)S(1)} %bitcast.6), dimensions={0,1} | broadcast | bytes 132096 | tf_op jit(solution)/shard_map/broadcast_in_dim | solution.py:407
  22.7 5.0 %all-to-all-start.1 = ((s32[32,8,128]{2,1,0:T(8,128)}), s32[32,8,128]{2,1,0:T(8,128)S(1)}, u32[]{:S(2)}, u32[]{:S(2)}) async-start(s32[32,8,128]{2,1,0:T(8,128)} %broadcast_in_dim.14), calls=%async_computation.1 | async-start | bytes 262144 | tf_op jit(solution)/shard_map/all_to_all | solution.py:410
  27.6 0.0 collective-permute-done.2.refs_0_
  27.6 0.0 collective-permute-done.3.refs_1_
  27.6 0.2 merge.3
  27.9 2.7 %collective-permute-start.4 = (s16[400,128]{1,0:T(8,128)(2,1)S(1)}, s16[400,128]{1,0:T(8,128)(2,1)S(1)}, u32[]{:S(2)}, u32[]{:S(2)}) collective-permute-start(s16[400,128]{1,0:T(8,128)(2,1)S(1)} %get-tuple-element.23), channel_id=1, source_target_pairs={{0,16},{4,20},{8,24},{12,28},{16,0},{20,4},{24,8},{28,12},{1,17},{... | collective-permute-start | bytes 307208 | tf_op jit(solution)/shard_map/ppermute | solution.py:398
  30.6 0.0 copy-done.3
  30.7 0.1 copy.7
  30.8 0.1 reshape.7.proj_ref
  30.9 7.7 %collective-permute-done.4.got_ref = s16[400,128]{1,0:T(8,128)(2,1)S(1)} collective-permute-done((s16[400,128]{1,0:T(8,128)(2,1)S(1)}, s16[400,128]{1,0:T(8,128)(2,1)S(1)}, u32[]{:S(2)}, u32[]{:S(2)}) %collective-permute-start.4) | collective-permute-done | bytes 102432 | tf_op jit(solution)/shard_map/ppermute | solution.py:398
  38.6 0.0 copy-done.1
  38.6 3.8 %sources.1 = f32[32,4,128]{2,1,0:T(4,128)S(1)} custom-call(f32[384]{0:T(512)S(1)} %reshape.7.proj_ref, s16[400,128]{1,0:T(8,128)(2,1)S(1)} %collective-permute-done.4.got_ref, f32[384,128]{1,0:T(8,128)S(1)} %get-tuple-element.24.kept_ref, bf16[64,64,128]{2,1,0:T(8,128)(2,1)S(1)} %bitcast.4), custom_call_target="tpu_custom_call" | custom-call | tf_op jit(solution)/shard_map/sources/pallas_call | solution.py:326
  42.4 0.0 all-to-all-done.1.delay_ref
  42.4 10.8 %all_to_all.10.got_ref = f32[32,4,128]{2,1,0:T(4,128)S(1)} all-to-all(f32[32,4,128]{2,1,0:T(4,128)S(1)} %sources.1), channel_id=1, replica_groups=mesh['blk'=8,'tm'=4] {'blk','tm'}, dimensions={0} | all-to-all | bytes 131072 | tf_op jit(solution)/shard_map/all_to_all | solution.py:430
  53.3 1.2 %records.1 = f32[8,64]{1,0:T(8,128)} custom-call(f32[32,4,128]{2,1,0:T(4,128)S(1)} %all_to_all.10.got_ref, s32[32,8,128]{2,1,0:T(8,128)S(1)} %all-to-all-done.1.delay_ref), custom_call_target="tpu_custom_call" | custom-call | tf_op jit(solution)/shard_map/records/pallas_call | solution.py:381
  (3 shorter events, 0.0 us)
Async XLA Ops:
  0.0 21.2 %copy-start.4 = (s32[64,1]{0,1:T(1,128)S(1)}, s32[64,1]{0,1:T(1,128)}, u32[]{:S(2)}) copy-start(s32[64,1]{0,1:T(1,128)} %param.11) | copy-start | bytes 772
  0.0 1.4 %copy-start = (bf16[96,64,128]{2,1,0:T(8,128)(2,1)S(1)}, bf16[96,64,128]{2,1,0:T(8,128)(2,1)}, u32[]{:S(2)}) copy-start(bf16[96,64,128]{2,1,0:T(8,128)(2,1)} %density_ref.1) | copy-start | bytes 4718596
  1.4 0.7 %copy-start.2 = (s32[96,1]{0,1:T(1,128)S(1)}, s32[96,1]{0,1:T(1,128)}, u32[]{:S(2)}) copy-start(s32[96,1]{0,1:T(1,128)} %param.8) | copy-start | bytes 1156
  2.1 28.5 %copy-start.3 = (f32[64,3]{0,1:T(4,128)S(1)}, f32[64,3]{0,1:T(4,128)}, u32[]{:S(2)}) copy-start(f32[64,3]{0,1:T(4,128)} %param.10) | copy-start | bytes 2308
  2.1 36.5 %copy-start.1 = (bf16[1,64,64,128]{3,2,1,0:T(8,128)(2,1)S(1)}, bf16[1,64,64,128]{3,2,1,0:T(8,128)(2,1)}, u32[]{:S(2)}) copy-start(bf16[1,64,64,128]{3,2,1,0:T(8,128)(2,1)} %param.9) | copy-start | bytes 3145732
  8.4 8.1 %collective-permute-start = (s16[784,128]{1,0:T(8,128)(2,1)S(1)}, s16[784,128]{1,0:T(8,128)(2,1)S(1)}, u32[]{:S(2)}, u32[]{:S(2)}) collective-permute-start(s16[784,128]{1,0:T(8,128)(2,1)S(1)} %get-tuple-element.15), channel_id=1, source_target_pairs={{0,4},{4,0},{8,12},{12,8},{16,20},{20,16},{24,28},{28,24},{1,5},{5... | collective-permute-start | bytes 602120 | tf_op jit(solution)/shard_map/ppermute | solution.py:398
  11.5 6.4 %collective-permute-start.1 = (s16[784,128]{1,0:T(8,128)(2,1)S(1)}, s16[784,128]{1,0:T(8,128)(2,1)S(1)}, u32[]{:S(2)}, u32[]{:S(2)}) collective-permute-start(s16[784,128]{1,0:T(8,128)(2,1)S(1)} %get-tuple-element.16), channel_id=1, source_target_pairs={{0,8},{4,12},{8,0},{12,4},{16,24},{20,28},{24,16},{28,20},{1,9},{5... | collective-permute-start | bytes 602120 | tf_op jit(solution)/shard_map/ppermute | solution.py:398
  18.5 9.2 %collective-permute-start.2 = (s16[400,128]{1,0:T(8,128)(2,1)S(1)}, s16[400,128]{1,0:T(8,128)(2,1)S(1)}, u32[]{:S(2)}, u32[]{:S(2)}) collective-permute-start(s16[400,128]{1,0:T(8,128)(2,1)S(1)} %get-tuple-element.19), channel_id=1, source_target_pairs={{0,8},{4,12},{8,0},{12,4},{16,24},{20,28},{24,16},{28,20},{1,9},{5... | collective-permute-start | bytes 307208 | tf_op jit(solution)/shard_map/ppermute | solution.py:398
  20.0 7.7 %collective-permute-start.3 = (s16[400,128]{1,0:T(8,128)(2,1)S(1)}, s16[400,128]{1,0:T(8,128)(2,1)S(1)}, u32[]{:S(2)}, u32[]{:S(2)}) collective-permute-start(s16[400,128]{1,0:T(8,128)(2,1)S(1)} %get-tuple-element.20), channel_id=1, source_target_pairs={{0,4},{4,0},{8,12},{12,8},{16,20},{20,16},{24,28},{28,24},{1,5},{5... | collective-permute-start | bytes 307208 | tf_op jit(solution)/shard_map/ppermute | solution.py:398
  22.7 19.8 %all-to-all-start.1 = ((s32[32,8,128]{2,1,0:T(8,128)}), s32[32,8,128]{2,1,0:T(8,128)S(1)}, u32[]{:S(2)}, u32[]{:S(2)}) async-start(s32[32,8,128]{2,1,0:T(8,128)} %broadcast_in_dim.14), calls=%async_computation.1 | async-start | bytes 262144 | tf_op jit(solution)/shard_map/all_to_all | solution.py:410
  27.9 10.7 %collective-permute-start.4 = (s16[400,128]{1,0:T(8,128)(2,1)S(1)}, s16[400,128]{1,0:T(8,128)(2,1)S(1)}, u32[]{:S(2)}, u32[]{:S(2)}) collective-permute-start(s16[400,128]{1,0:T(8,128)(2,1)S(1)} %get-tuple-element.23), channel_id=1, source_target_pairs={{0,16},{4,20},{8,24},{12,28},{16,0},{20,4},{24,8},{28,12},{1,17},{... | collective-permute-start | bytes 307208 | tf_op jit(solution)/shard_map/ppermute | solution.py:398

commit v2 on v0

v2 whole, which is shorter than its diff:
```python
import functools

import jax
import jax.numpy as jnp
from jax import lax
from jax.experimental import pallas as pl
from jax.experimental.pallas import tpu as pltpu
from jax.sharding import PartitionSpec as P

COMPS = 6
TILE = 16
LANES = 128
GROUP = 8
UNROLL = 4
GRAIN = 128.0
TOP = 32764.0
FLOOR = 1e-35


def whole():
    return pl.BlockSpec(memory_space=pltpu.VMEM)


def scalars():
    return pl.BlockSpec(memory_space=pltpu.SMEM)


def params(mebibytes=40):
    return pltpu.CompilerParams(vmem_limit_bytes=mebibytes * 1024 * 1024)


def scale_code(largest):
    return jnp.ceil(jnp.log(jnp.maximum(largest, FLOOR)) * GRAIN)


def encode(values, inverse):
    return jnp.round(values * inverse).astype(jnp.int32).astype(jnp.int16)


def encode_factor(code):
    return jnp.exp(code * (-1.0 / GRAIN)) * TOP


def decode_factor(code16):
    code = code16.astype(jnp.int32).astype(jnp.float32)
    return jnp.exp(code * (1.0 / GRAIN)) * (1.0 / TOP)


def decode(code16, factor):
    return code16.astype(jnp.int32).astype(jnp.float32) * factor


def with_bit(index, position, bit):
    low = index & ((1 << position) - 1)
    return ((index >> position) << (position + 1)) | (bit << position) | low


def rows_at(start, size=TILE):
    return pl.ds(pl.multiple_of(start, TILE), size)


def write_codes(largest, staged, send_ref, rows):
    code = scale_code(largest)
    inverse = encode_factor(code)

    def step(k, carry):
        where = rows_at(k * TILE)
        send_ref[where, :] = encode(staged[where, :], inverse)
        return carry

    lax.fori_loop(0, rows // TILE, step, 0, unroll=4)
    send_ref[rows:rows + TILE, :] = code.astype(jnp.int32).astype(jnp.int16)


def bucket(blocks, rows, dest_ref, counts, members):
    stride = rows + UNROLL

    def clear(b, carry):
        counts[b] = 0
        return carry

    lax.fori_loop(0, blocks, clear, 0)

    def place(r, carry):
        target = dest_ref[r]
        count = counts[target]
        members[target * stride + count] = r
        counts[target] = count + 1
        return carry

    lax.fori_loop(0, rows, place, 0, unroll=4)

    def pad(b, carry):
        end = b * stride + counts[b]
        for extra in range(UNROLL - 1):
            members[end + extra] = rows
        return carry

    lax.fori_loop(0, blocks, pad, 0)


def block_sums(target, at, stride, dens, flow, counts, members):
    first = target * stride

    def body(turn, totals):
        totals = list(totals)
        for u in range(UNROLL):
            row = members[first + turn * UNROLL + u]
            rho = dens[row, at, :].astype(jnp.float32)
            ux = flow[row, 0, at, :].astype(jnp.float32)
            uy = flow[row, 1, at, :].astype(jnp.float32)
            uz = flow[row, 2, at, :].astype(jnp.float32)
            excess = flow[row, 3, at, :].astype(jnp.float32)
            mx, my, mz = rho * ux, rho * uy, rho * uz
            for i, term in enumerate((mx * ux, my * uy, mz * uz, mx * uy, mx * uz, my * uz, excess)):
                totals[i] = totals[i] + term
        return tuple(totals)

    zero = jnp.zeros((TILE, LANES), jnp.float32)
    turns = (counts[target] + (UNROLL - 1)) // UNROLL
    xx, yy, zz, xy, xz, yz, excess = lax.fori_loop(0, turns, body, (zero,) * 7)
    return xx + excess, yy + excess, zz + excess, xy, xz, yz


def stress_kernel(blocks, bits, leaving, dest_ref, density_ref, flow_ref, *refs):
    halves = len(bits)
    outs, (dens, flow, dest, counts, members, staged, sems, dest_sem) = refs[:halves], refs[halves:]
    rows, steps = density_ref.shape[0], density_ref.shape[1]
    tiles = steps // TILE
    per_half = tiles // halves
    span = steps // halves
    fetch = pltpu.make_async_copy(dest_ref, dest, dest_sem)
    fetch.start()
    copies = []
    for k in range(tiles):
        at = pl.ds(k * TILE, TILE)
        pair = (
            pltpu.make_async_copy(density_ref.at[:, at, :], dens.at[pl.ds(0, rows), at, :], sems.at[k, 0]),
            pltpu.make_async_copy(flow_ref.at[:, :, at, :], flow.at[pl.ds(0, rows), :, at, :], sems.at[k, 1]),
        )
        for copy in pair:
            copy.start()
        copies.append(pair)

    dens[rows] = jnp.zeros_like(dens[rows])
    flow[rows] = jnp.zeros_like(flow[rows])
    fetch.wait()
    bucket(blocks, rows, dest, counts, members)
    me = lax.axis_index("blk")
    for half in range(halves):
        target_ref = staged if leaving else outs[half]
        largest = jnp.zeros((TILE, LANES), jnp.float32)
        for k in range(per_half):
            tile = half * per_half + k
            at = slice(tile * TILE, (tile + 1) * TILE)
            for copy in copies[tile]:
                copy.wait()

            def block(i, top):
                target = me ^ with_bit(i, bits[half], int(leaving))
                pieces = block_sums(target, at, rows + UNROLL, dens, flow, counts, members)
                for c, piece in enumerate(pieces):
                    target_ref[rows_at((i * COMPS + c) * span + k * TILE), :] = piece
                    if leaving:
                        top = jnp.maximum(top, jnp.abs(piece))
                return top

            largest = lax.fori_loop(0, blocks // 2, block, largest)
        if leaving:
            write_codes(largest, staged, outs[half], blocks // 2 * COMPS * span)


def stress_sums(density, flow_rest, targets, blocks, bits, leaving):
    rows, steps, _ = density.shape
    halves = len(bits)
    size = blocks // 2 * COMPS * (steps // halves)
    if leaving:
        out = jax.ShapeDtypeStruct((size + TILE, LANES), jnp.int16)
    else:
        out = jax.ShapeDtypeStruct((size, LANES), jnp.float32)
    return pl.pallas_call(
        functools.partial(stress_kernel, blocks, bits, leaving),
        out_shape=[out] * halves,
        in_specs=[pl.BlockSpec(memory_space=pl.ANY)] * 3,
        out_specs=[whole()] * halves,
        scratch_shapes=[
            pltpu.VMEM((rows + 1, steps, LANES), density.dtype),
            pltpu.VMEM((rows + 1, flow_rest.shape[1], steps, LANES), flow_rest.dtype),
            pltpu.SMEM((rows,), jnp.int32),
            pltpu.SMEM((blocks,), jnp.int32),
            pltpu.SMEM((blocks * (rows + UNROLL),), jnp.int32),
            pltpu.VMEM((size if leaving else TILE, LANES), jnp.float32),
            pltpu.SemaphoreType.DMA((steps // TILE, 2)),
            pltpu.SemaphoreType.DMA(()),
        ],
        compiler_params=params(58 if leaving else 50),
        name="leaving_sums" if leaving else "staying_sums",
    )(targets, density, flow_rest)


def merge_kernel(count, positions, size, messages, *refs):
    halves = len(positions)
    got, kept = refs[:messages], refs[messages:messages + halves]
    send, keeps, staged = refs[messages + halves], refs[messages + halves + 1:-1], refs[-1]
    half = count // 2
    largest = jnp.zeros((TILE, LANES), jnp.float32)
    for p in range(halves):
        message = got[min(p, messages - 1)]
        offset = (p if messages < halves else 0) * count * size
        factor = decode_factor(message[message.shape[0] - TILE:, :])

        def total(block, k):
            where = block * size + k * TILE
            return kept[p][rows_at(where), :] + decode(message[rows_at(offset + where), :], factor)

        def sent(i, top):
            def tile(k, top):
                piece = total(with_bit(i, positions[p], 1), k)
                staged[rows_at((p * half + i) * size + k * TILE), :] = piece
                return jnp.maximum(top, jnp.abs(piece))

            return lax.fori_loop(0, size // TILE, tile, top, unroll=4)

        largest = lax.fori_loop(0, half, sent, largest)

        def stay(i, carry):
            def tile(k, carry):
                keeps[p][rows_at(i * size + k * TILE), :] = total(with_bit(i, positions[p], 0), k)
                return carry

            return lax.fori_loop(0, size // TILE, tile, carry, unroll=4)

        lax.fori_loop(0, half, stay, 0)
    write_codes(largest, staged, send, halves * half * size)


def merge(got, kept, count, positions, size):
    rows = count // 2 * size
    halves = len(kept)
    made = pl.pallas_call(
        functools.partial(merge_kernel, count, tuple(positions), size, len(got)),
        out_shape=[jax.ShapeDtypeStruct((halves * rows + TILE, LANES), jnp.int16)]
        + [jax.ShapeDtypeStruct((rows, LANES), jnp.float32)] * halves,
        in_specs=[whole()] * (len(got) + halves),
        out_specs=[whole()] * (1 + halves),
        scratch_shapes=[pltpu.VMEM((halves * rows, LANES), jnp.float32)],
        compiler_params=params(),
        name="merge",
    )(*got, *kept)
    return made[0], list(made[1:])


def project(half, got_ref, kept_ref, proj_ref, weights_ref, totals):
    observers = weights_ref.shape[0]
    span = kept_ref.shape[0] // COMPS
    factor = decode_factor(got_ref[COMPS * span:COMPS * span + TILE, :])

    def fill(k, carry):
        where = rows_at(k * TILE)
        totals[where, :] = kept_ref[where, :] + decode(got_ref[where, :], factor)
        return carry

    lax.fori_loop(0, COMPS * span // TILE, fill, 0, unroll=4)
    lane = lax.broadcasted_iota(jnp.int32, (span, LANES), 1) % observers
    ones = jnp.ones((2 * LANES, LANES), jnp.bfloat16)
    at = slice(half * span, (half + 1) * span)
    parts = [totals[c * span:(c + 1) * span, :] for c in range(COMPS)]
    value = jnp.zeros((span, LANES), jnp.float32)
    for group in range(0, observers, GROUP):
        rows = []
        for o in range(group, group + GROUP):
            moment = proj_ref[o:o + 1, :] * parts[0]
            for c in range(1, COMPS):
                moment = moment + proj_ref[c * observers + o:c * observers + o + 1, :] * parts[c]
            term = weights_ref[o, at, :].astype(jnp.float32) * moment
            high = term.astype(jnp.bfloat16)
            low = (term - high.astype(jnp.float32)).astype(jnp.bfloat16)
            rows.append(jnp.concatenate([high, low], axis=1))
        sums = jnp.dot(jnp.concatenate(rows, axis=0), ones, preferred_element_type=jnp.float32)
        for u in range(GROUP):
            value = jnp.where(lane == group + u, sums[u * span:(u + 1) * span], value)
    return value


def first_kernel(proj_ref, got_ref, kept_ref, weights_ref, out_ref, totals):
    out_ref[...] = project(0, got_ref, kept_ref, proj_ref, weights_ref, totals)


def last_kernel(slabs, per_device, proj_ref, got_ref, kept_ref, weights_ref, first_ref, bins_ref, out_ref, totals):
    observers, steps, _ = weights_ref.shape
    source = jnp.concatenate(
        [first_ref[...], project(1, got_ref, kept_ref, proj_ref, weights_ref, totals)], axis=0
    )
    across = jnp.concatenate([source] * (LANES // steps), axis=0).T[:observers]
    period = slabs * steps
    lane = lax.broadcasted_iota(jnp.int32, (observers, LANES), 1)
    blank = jnp.zeros((observers, LANES), jnp.float32)
    value = jnp.concatenate([jnp.where(lane < steps, across, blank)] + [blank] * (period // LANES - 1), axis=1)
    value = pltpu.roll(value, period - 1, 1) - 2.0 * value + pltpu.roll(value, 1, 1)
    delay = bins_ref[...] + lax.axis_index("tm") * steps
    delay = jnp.where(delay >= period, delay - period, delay)
    shift = 1
    while shift < period:
        value = jnp.where((delay & shift) != 0, pltpu.roll(value, shift, 1), value)
        shift *= 2
    rows = out_ref.shape[1]
    lane = lax.broadcasted_iota(jnp.int32, (per_device, LANES), 1)
    low = lane < steps
    for b in range(observers // per_device):
        for pair in range(period // LANES):
            mine = value[b * per_device:(b + 1) * per_device, pair * LANES:(pair + 1) * LANES]
            turned = pltpu.roll(mine, steps, 1)
            if rows < per_device:
                down = jnp.concatenate([mine[rows:], mine[:rows]], axis=0)
                down_turned = jnp.concatenate([turned[rows:], turned[:rows]], axis=0)
                out_ref[b * slabs + 2 * pair] = jnp.where(low, mine, down_turned)[:rows]
                out_ref[b * slabs + 2 * pair + 1] = jnp.where(low, turned, down)[:rows]
            else:
                out_ref[b * slabs + 2 * pair] = mine
                out_ref[b * slabs + 2 * pair + 1] = turned


def sources(projector, got, kept, weights, bins, blocks, slabs):
    observers = weights.shape[0]
    per_device = observers // blocks
    rows = per_device // 2 if per_device % 2 == 0 else per_device
    size = kept[0].shape[0]
    first = pl.pallas_call(
        first_kernel,
        out_shape=jax.ShapeDtypeStruct((size // COMPS, LANES), jnp.float32),
        in_specs=[whole()] * 4,
        out_specs=whole(),
        scratch_shapes=[pltpu.VMEM((size, LANES), jnp.float32)],
        compiler_params=params(),
        name="first_sources",
    )(projector, got[0], kept[0], weights)
    return pl.pallas_call(
        functools.partial(last_kernel, slabs, per_device),
        out_shape=jax.ShapeDtypeStruct((blocks * slabs, rows, LANES), jnp.float32),
        in_specs=[whole()] * 6,
        out_specs=whole(),
        scratch_shapes=[pltpu.VMEM((size, LANES), jnp.float32)],
        compiler_params=params(),
        name="last_sources",
    )(projector, got[1], kept[1], weights, first, bins)


def record_kernel(got_ref, out_ref):
    per_device, steps = out_ref.shape
    total = got_ref[0]
    for k in range(1, got_ref.shape[0]):
        total = total + got_ref[k]
    rows = total.shape[0]
    out_ref[:rows, :] = total[:, :steps]
    if rows < per_device:
        out_ref[rows:, :] = total[:, steps:]


def records(got, per_device, steps):
    return pl.pallas_call(
        record_kernel,
        out_shape=jax.ShapeDtypeStruct((per_device, steps), jnp.float32),
        in_specs=[whole()],
        out_specs=whole(),
        compiler_params=params(),
        name="records",
    )(got)


def body(density, flow_rest, dest, weights, directions, bins):
    blocks, slabs = lax.axis_size("blk"), lax.axis_size("tm")
    steps = density.shape[1]
    observers = bins.shape[0]

    def swap(values, bit):
        return lax.ppermute(values, "blk", [(i, i ^ (1 << bit)) for i in range(blocks)])

    stages = blocks.bit_length() - 1
    orders = [list(range(stages)) for _ in range(2)]
    orders[1][:2] = [1, 0]
    size = COMPS * (steps // 2)
    bits = tuple(order[0] for order in orders)
    sends = stress_sums(density, flow_rest, dest[:, 0], blocks, bits, True)
    kept = stress_sums(density, flow_rest, dest[:, 0], blocks, bits, False)
    got = [swap(send, order[0]) for send, order in zip(sends, orders)]
    count = blocks // 2
    for stage in range(1, stages):
        places = [sorted(order[stage:]).index(order[stage]) for order in orders]
        made = [merge(got[p:p + 1], kept[p:p + 1], count, places[p:p + 1], size) for p in range(2)]
        got = [swap(made[p][0], orders[p][stage]) for p in range(2)]
        kept = made[0][1] + made[1][1]
        count //= 2

    d1, d2, d3 = [jnp.broadcast_to(directions[:, c:c + 1], (observers, LANES)) for c in range(3)]
    projector = jnp.concatenate(
        [d1 * d1, d2 * d2, d3 * d3, 2.0 * d1 * d2, 2.0 * d1 * d3, 2.0 * d2 * d3], axis=0
    )
    chunks = sources(projector, got, kept, weights[0], bins, blocks, slabs)
    chunks = lax.all_to_all(chunks, ("blk", "tm"), split_axis=0, concat_axis=0, tiled=True)
    return records(chunks, observers // blocks, steps)


def solution(mesh):
    placed = (
        P("blk", "tm", None),
        P("blk", None, "tm", None),
        P("blk", None),
        P("blk", None, "tm", None),
        P(),
        P(None, "blk"),
    )
    return jax.shard_map(
        body, mesh=mesh, in_specs=placed, out_specs=P("blk", "tm"), check_vma=False
    )
```

time: 153 us -> 40.3 us (0.26)
  local copies, waits for them, and re-layouts: 40.4 us -> 0.54 us
  waiting for transfers between devices: 35.5 us -> 4.22 us
  blocking collectives: 40.6 us -> 11 us
  other arithmetic: 15.8 us -> 0.01 us
  Pallas kernels: 0 us -> 12.4 us
  matrix products: 12 us -> 0 us
  starting transfers between devices: 7.4 us -> 11.9 us
    all_to_all x1 -> x0, waiting for transfers between devices: 35.5 us -> none  [body(): lax.all_to_all(grouped, 'blk', split_axis=0, concat_axis=0, tiled=True)]
    unnamed x1 -> x0, blocking collectives: 35.2 us -> none
    gather x3 -> x0, local copies, waits for them, and re-layouts: 32.9 us -> none  [body(): shifted = jnp.take_along_axis(curved, lagged, axis=1)]
    unnamed x5 -> x0, other arithmetic: 12.9 us -> none
    pallas_call x0 -> x9, Pallas kernels: none -> 12.4 us  [the longest x2 8.61 us: stress_sums(): pl.pallas_call(functools.partial(stress_kernel, blocks, bits, leaving), o...]
    dot_general x2 -> x0, matrix products: 12 us -> none  [the longest x1 9.23 us: body(): jnp.einsum('br,ritc->bitc', membership, stresses, precision=lax.Precision...]
    ppermute x0 -> x6, starting transfers between devices: none -> 11.9 us  [swap(): lax.ppermute(values, 'blk', [(i, i ^ 1 << bit) for i in range(blocks)])]
    all_to_all x0 -> x1, blocking collectives: none -> 11 us  [body(): lax.all_to_all(chunks, ('blk', 'tm'), split_axis=0, concat_axis=0, tiled=...]
  transfers between devices with their start and end apart: 1 -> 6, of which waited for: 1 -> 3; matrix products, arithmetic and copies ran while one was open for 1% -> 1% of each run, Pallas kernels for 0% -> 13%
where the time goes in v2:
time: 40.3 us; the launch traced here: 40.1 us
  Pallas kernels  12.4 us (31%)
  starting transfers between devices  11.9 us (30%)
  blocking collectives  11 us (27%)
  waiting for transfers between devices  4.22 us (10%)
  local copies, waits for them, and re-layouts  0.54 us (1%)
    ppermute x6, starting transfers between devices, swap(): lax.ppermute(values, 'blk', [(i, i ^ 1 << bit) for i in range(blocks)])  11.9 us
    all_to_all x1, blocking collectives, body(): lax.all_to_all(chunks, ('blk', 'tm'), split_axis=0, concat_axis=0, tiled=...  11 us
    pallas_call x2, Pallas kernels, stress_sums(): pl.pallas_call(functools.partial(stress_kernel, blocks, bits, leaving), o...  8.61 us
    ppermute x6, waiting for transfers between devices, swap(): lax.ppermute(values, 'blk', [(i, i ^ 1 << bit) for i in range(blocks)])  4.22 us
    pallas_call x1, Pallas kernels, sources(): pl.pallas_call(functools.partial(last_kernel, slabs, per_device), out_sha...  1.52 us
  transfers between devices with their start and end apart: 6, of which 3 were waited for; matrix products, arithmetic and copies ran while one was open for 1% of the time, Pallas kernels for 13%

profile of v2, /device:TPU:0, one launch (start us, length us, event | category | flops | bytes accessed | tf_op | source)
XLA Modules:
  0.0 40.1 jit_solution(3466356618606530353)
XLA Ops:
  0.0 0.0 copy-start.2
  0.0 0.0 copy-start
  0.0 0.0 copy-start.3
  0.0 4.8 %leaving_sums.1 = (s16[784,128]{1,0:T(8,128)(2,1)}, s16[784,128]{1,0:T(8,128)(2,1)}) custom-call(s32[96]{0:T(128)} %bitcast.19, bf16[96,64,128]{2,1,0:T(8,128)(2,1)} %density_ref.3, bf16[96,4,64,128]{3,2,1,0:T(8,128)(2,1)} %flow_ref.3), custom_call_target="tpu_custom_call" | custom-call | tf_op jit(solution)/shard_map/leaving_sums/pallas_call | solution.py:181
  4.9 0.0 copy-start.4
  4.9 0.0 copy-start.1
  4.9 3.0 %collective-permute-start.3 = (s16[784,128]{1,0:T(8,128)(2,1)}, s16[784,128]{1,0:T(8,128)(2,1)S(1)}, u32[]{:S(2)}, u32[]{:S(2)}) collective-permute-start(s16[784,128]{1,0:T(8,128)(2,1)} %get-tuple-element.23), channel_id=1, source_target_pairs={{0,4},{4,0},{8,12},{12,8},{16,20},{20,16},{24,28},{28,24},{1,5},{5... | collective-permute-start | bytes 602120 | tf_op jit(solution)/shard_map/ppermute | solution.py:376
  7.9 1.7 %collective-permute-start = (s16[784,128]{1,0:T(8,128)(2,1)}, s16[784,128]{1,0:T(8,128)(2,1)S(1)}, u32[]{:S(2)}, u32[]{:S(2)}) collective-permute-start(s16[784,128]{1,0:T(8,128)(2,1)} %get-tuple-element.17), channel_id=1, source_target_pairs={{0,8},{4,12},{8,0},{12,4},{16,24},{20,28},{24,16},{28,20},{1,9},{5... | collective-permute-start | bytes 602120 | tf_op jit(solution)/shard_map/ppermute | solution.py:376
  9.7 0.0 copy-done.3
  9.7 0.0 copy-done.2
  9.7 0.0 copy-done
  9.7 3.8 %staying_sums.1 = (f32[768,128]{1,0:T(8,128)S(1)}, f32[768,128]{1,0:T(8,128)S(1)}) custom-call(s32[96]{0:T(128)S(1)} %bitcast.20, bf16[96,64,128]{2,1,0:T(8,128)(2,1)S(1)} %copy-done, bf16[96,4,64,128]{3,2,1,0:T(8,128)(2,1)} %flow_ref.3), custom_call_target="tpu_custom_call" | custom-call | tf_op jit(solution)/shard_map/staying_sums/pallas_call | solution.py:181
  13.5 0.1 broadcast_dynamic-update-slice_fusion.5
  13.5 0.1 broadcast_dynamic-update-slice_fusion.4
  13.6 0.1 broadcast_dynamic-update-slice_fusion.3
  13.7 0.1 broadcast_dynamic-update-slice_fusion.2
  13.8 0.0 collective-permute-done.3.refs_0_
  13.8 0.3 merge.6
  14.1 1.3 %collective-permute-start.4 = (s16[400,128]{1,0:T(8,128)(2,1)S(1)}, s16[400,128]{1,0:T(8,128)(2,1)S(1)}, u32[]{:S(2)}, u32[]{:S(2)}) collective-permute-start(s16[400,128]{1,0:T(8,128)(2,1)S(1)} %get-tuple-element.25), channel_id=1, source_target_pairs={{0,8},{4,12},{8,0},{12,4},{16,24},{20,28},{24,16},{28,20},{1,9},{5... | collective-permute-start | bytes 307208 | tf_op jit(solution)/shard_map/ppermute | solution.py:376
  15.3 0.0 collective-permute-done.refs_0_
  15.3 0.3 merge.4
  15.6 1.7 %collective-permute-start.1 = (s16[400,128]{1,0:T(8,128)(2,1)S(1)}, s16[400,128]{1,0:T(8,128)(2,1)S(1)}, u32[]{:S(2)}, u32[]{:S(2)}) collective-permute-start(s16[400,128]{1,0:T(8,128)(2,1)S(1)} %get-tuple-element.19), channel_id=1, source_target_pairs={{0,4},{4,0},{8,12},{12,8},{16,20},{20,16},{24,28},{28,24},{1,5},{5... | collective-permute-start | bytes 307208 | tf_op jit(solution)/shard_map/ppermute | solution.py:376
  17.3 0.1 broadcast_dynamic-update-slice_fusion.1
  17.3 1.4 %collective-permute-done.4.refs_0_ = s16[400,128]{1,0:T(8,128)(2,1)S(1)} collective-permute-done((s16[400,128]{1,0:T(8,128)(2,1)S(1)}, s16[400,128]{1,0:T(8,128)(2,1)S(1)}, u32[]{:S(2)}, u32[]{:S(2)}) %collective-permute-start.4) | collective-permute-done | bytes 102432 | tf_op jit(solution)/shard_map/ppermute | solution.py:376
  18.8 0.1 merge.7
  18.9 2.8 %collective-permute-start.5 = (s16[208,128]{1,0:T(8,128)(2,1)S(1)}, s16[208,128]{1,0:T(8,128)(2,1)S(1)}, u32[]{:S(2)}, u32[]{:S(2)}) collective-permute-start(s16[208,128]{1,0:T(8,128)(2,1)S(1)} %get-tuple-element.27), channel_id=1, source_target_pairs={{0,16},{4,20},{8,24},{12,28},{16,0},{20,4},{24,8},{28,12},{1,17},{... | collective-permute-start | bytes 159752 | tf_op jit(solution)/shard_map/ppermute | solution.py:376
  21.7 0.0 collective-permute-done.1.refs_0_
  21.7 0.1 merge.5
  21.8 1.4 %collective-permute-start.2 = (s16[208,128]{1,0:T(8,128)(2,1)S(1)}, s16[208,128]{1,0:T(8,128)(2,1)S(1)}, u32[]{:S(2)}, u32[]{:S(2)}) collective-permute-start(s16[208,128]{1,0:T(8,128)(2,1)S(1)} %get-tuple-element.21), channel_id=1, source_target_pairs={{0,16},{4,20},{8,24},{12,28},{16,0},{20,4},{24,8},{28,12},{1,17},{... | collective-permute-start | bytes 159752 | tf_op jit(solution)/shard_map/ppermute | solution.py:376
  23.2 0.1 broadcast_dynamic-update-slice_fusion.proj_ref
  23.3 0.0 copy-done.4
  23.3 0.1 copy.7.bins_ref
  23.4 2.1 %collective-permute-done.5.got_ref = s16[208,128]{1,0:T(8,128)(2,1)S(1)} collective-permute-done((s16[208,128]{1,0:T(8,128)(2,1)S(1)}, s16[208,128]{1,0:T(8,128)(2,1)S(1)}, u32[]{:S(2)}, u32[]{:S(2)}) %collective-permute-start.5) | collective-permute-done | bytes 53280 | tf_op jit(solution)/shard_map/ppermute | solution.py:376
  25.5 0.0 copy-done.1
  25.5 0.8 %first_sources.1.first_ref = f32[32,128]{1,0:T(8,128)S(1)} custom-call(f32[384,128]{1,0:T(8,128)S(1)} %broadcast_dynamic-update-slice_fusion.proj_ref, s16[208,128]{1,0:T(8,128)(2,1)S(1)} %collective-permute-done.5.got_ref, f32[192,128]{1,0:T(8,128)S(1)} %get-tuple-element.28.kept_ref, bf16[64,64,128]{2,1,0:T(8,128)(2,1)S(1)} %bitcast.17), custom_call_target="tpu_custom_call" | custom-call | tf_op jit(solution)/shard_map/first_sources/pallas_call | solution.py:328
  26.3 0.6 %collective-permute-done.2.got_ref = s16[208,128]{1,0:T(8,128)(2,1)S(1)} collective-permute-done((s16[208,128]{1,0:T(8,128)(2,1)S(1)}, s16[208,128]{1,0:T(8,128)(2,1)S(1)}, u32[]{:S(2)}, u32[]{:S(2)}) %collective-permute-start.2) | collective-permute-done | bytes 53280 | tf_op jit(solution)/shard_map/ppermute | solution.py:376
  26.9 1.5 %last_sources.1 = f32[32,4,128]{2,1,0:T(4,128)S(1)} custom-call(f32[384,128]{1,0:T(8,128)S(1)} %broadcast_dynamic-update-slice_fusion.proj_ref, s16[208,128]{1,0:T(8,128)(2,1)S(1)} %collective-permute-done.2.got_ref, f32[192,128]{1,0:T(8,128)S(1)} %get-tuple-element.22.kept_ref, bf16[64,64,128]{2,1,0:T(8,128)(2,1)S(1)} %bitcast.18, ...), custom_call_target="tpu_custom_call" | custom-call | tf_op jit(solution)/shard_map/last_sources/pallas_call | solution.py:337
  28.4 11.0 %all_to_all.5.got_ref = f32[32,4,128]{2,1,0:T(4,128)S(1)} all-to-all(f32[32,4,128]{2,1,0:T(4,128)S(1)} %last_sources.1), channel_id=1, replica_groups=mesh['blk'=8,'tm'=4] {'blk','tm'}, dimensions={0} | all-to-all | bytes 131072 | tf_op jit(solution)/shard_map/all_to_all | solution.py:399
  39.4 0.7 %records.1 = f32[8,64]{1,0:T(8,128)} custom-call(f32[32,4,128]{2,1,0:T(4,128)S(1)} %all_to_all.5.got_ref), custom_call_target="tpu_custom_call" | custom-call | tf_op jit(solution)/shard_map/records/pallas_call | solution.py:360
  (2 shorter events, 0.0 us)
Async XLA Ops:
  0.0 9.7 %copy-start.2 = (s32[96,1]{0,1:T(1,128)S(1)}, s32[96,1]{0,1:T(1,128)}, u32[]{:S(2)}) copy-start(s32[96,1]{0,1:T(1,128)} %param.8) | copy-start | bytes 1156
  0.0 9.7 %copy-start = (bf16[96,64,128]{2,1,0:T(8,128)(2,1)S(1)}, bf16[96,64,128]{2,1,0:T(8,128)(2,1)}, u32[]{:S(2)}) copy-start(bf16[96,64,128]{2,1,0:T(8,128)(2,1)} %density_ref.3) | copy-start | bytes 4718596
  0.0 9.7 %copy-start.3 = (f32[64,3]{0,1:T(4,128)S(1)}, f32[64,3]{0,1:T(4,128)}, u32[]{:S(2)}) copy-start(f32[64,3]{0,1:T(4,128)} %param.10) | copy-start | bytes 2308
  4.9 18.4 %copy-start.4 = (s32[64,1]{0,1:T(1,128)S(1)}, s32[64,1]{0,1:T(1,128)}, u32[]{:S(2)}) copy-start(s32[64,1]{0,1:T(1,128)} %param.11) | copy-start | bytes 772
  4.9 20.6 %copy-start.1 = (bf16[1,64,64,128]{3,2,1,0:T(8,128)(2,1)S(1)}, bf16[1,64,64,128]{3,2,1,0:T(8,128)(2,1)}, u32[]{:S(2)}) copy-start(bf16[1,64,64,128]{3,2,1,0:T(8,128)(2,1)} %param.9) | copy-start | bytes 3145732
  4.9 8.9 %collective-permute-start.3 = (s16[784,128]{1,0:T(8,128)(2,1)}, s16[784,128]{1,0:T(8,128)(2,1)S(1)}, u32[]{:S(2)}, u32[]{:S(2)}) collective-permute-start(s16[784,128]{1,0:T(8,128)(2,1)} %get-tuple-element.23), channel_id=1, source_target_pairs={{0,4},{4,0},{8,12},{12,8},{16,20},{20,16},{24,28},{28,24},{1,5},{5... | collective-permute-start | bytes 602120 | tf_op jit(solution)/shard_map/ppermute | solution.py:376
  7.9 7.4 %collective-permute-start = (s16[784,128]{1,0:T(8,128)(2,1)}, s16[784,128]{1,0:T(8,128)(2,1)S(1)}, u32[]{:S(2)}, u32[]{:S(2)}) collective-permute-start(s16[784,128]{1,0:T(8,128)(2,1)} %get-tuple-element.17), channel_id=1, source_target_pairs={{0,8},{4,12},{8,0},{12,4},{16,24},{20,28},{24,16},{28,20},{1,9},{5... | collective-permute-start | bytes 602120 | tf_op jit(solution)/shard_map/ppermute | solution.py:376
  14.1 4.7 %collective-permute-start.4 = (s16[400,128]{1,0:T(8,128)(2,1)S(1)}, s16[400,128]{1,0:T(8,128)(2,1)S(1)}, u32[]{:S(2)}, u32[]{:S(2)}) collective-permute-start(s16[400,128]{1,0:T(8,128)(2,1)S(1)} %get-tuple-element.25), channel_id=1, source_target_pairs={{0,8},{4,12},{8,0},{12,4},{16,24},{20,28},{24,16},{28,20},{1,9},{5... | collective-permute-start | bytes 307208 | tf_op jit(solution)/shard_map/ppermute | solution.py:376
  15.6 6.1 %collective-permute-start.1 = (s16[400,128]{1,0:T(8,128)(2,1)S(1)}, s16[400,128]{1,0:T(8,128)(2,1)S(1)}, u32[]{:S(2)}, u32[]{:S(2)}) collective-permute-start(s16[400,128]{1,0:T(8,128)(2,1)S(1)} %get-tuple-element.19), channel_id=1, source_target_pairs={{0,4},{4,0},{8,12},{12,8},{16,20},{20,16},{24,28},{28,24},{1,5},{5... | collective-permute-start | bytes 307208 | tf_op jit(solution)/shard_map/ppermute | solution.py:376
  18.9 6.6 %collective-permute-start.5 = (s16[208,128]{1,0:T(8,128)(2,1)S(1)}, s16[208,128]{1,0:T(8,128)(2,1)S(1)}, u32[]{:S(2)}, u32[]{:S(2)}) collective-permute-start(s16[208,128]{1,0:T(8,128)(2,1)S(1)} %get-tuple-element.27), channel_id=1, source_target_pairs={{0,16},{4,20},{8,24},{12,28},{16,0},{20,4},{24,8},{28,12},{1,17},{... | collective-permute-start | bytes 159752 | tf_op jit(solution)/shard_map/ppermute | solution.py:376
  21.8 5.1 %collective-permute-start.2 = (s16[208,128]{1,0:T(8,128)(2,1)S(1)}, s16[208,128]{1,0:T(8,128)(2,1)S(1)}, u32[]{:S(2)}, u32[]{:S(2)}) collective-permute-start(s16[208,128]{1,0:T(8,128)(2,1)S(1)} %get-tuple-element.21), channel_id=1, source_target_pairs={{0,16},{4,20},{8,24},{12,28},{16,0},{20,4},{24,8},{28,12},{1,17},{... | collective-permute-start | bytes 159752 | tf_op jit(solution)/shard_map/ppermute | solution.py:376

commit v3 on v2

--- a/solution.py
+++ b/solution.py
@@ -291,24 +291,39 @@
     source = jnp.concatenate(
         [first_ref[...], project(1, got_ref, kept_ref, proj_ref, weights_ref, totals)], axis=0
     )
-    across = jnp.concatenate([source] * (LANES // steps), axis=0).T[:observers]
-    period = slabs * steps
-    lane = lax.broadcasted_iota(jnp.int32, (observers, LANES), 1)
-    blank = jnp.zeros((observers, LANES), jnp.float32)
-    value = jnp.concatenate([jnp.where(lane < steps, across, blank)] + [blank] * (period // LANES - 1), axis=1)
-    value = pltpu.roll(value, period - 1, 1) - 2.0 * value + pltpu.roll(value, 1, 1)
-    delay = bins_ref[...] + lax.axis_index("tm") * steps
+    lead, period = 8, slabs * steps
+    blank = jnp.zeros((lead, LANES), jnp.float32)
+    value = jnp.concatenate([blank, source, blank], axis=0)
+    size = value.shape[0]
+    value = pltpu.roll(value, size - 1, 0) - 2.0 * value + pltpu.roll(value, 1, 0)
+    value = jnp.concatenate([value, blank], axis=0)
+    delay = bins_ref[...] + (lax.axis_index("tm") * steps + period - lead)
+    delay = jnp.broadcast_to(jnp.where(delay >= period, delay - period, delay), (lead, LANES))
     delay = jnp.where(delay >= period, delay - period, delay)
     shift = 1
-    while shift < period:
-        value = jnp.where((delay & shift) != 0, pltpu.roll(value, shift, 1), value)
+    while shift < lead:
+        late = jnp.concatenate([(delay & shift) != 0] * (value.shape[0] // lead), axis=0)
+        value = jnp.where(late, pltpu.roll(value, shift, 0), value)
         shift *= 2
+    tiles = [value[k:k + lead] for k in range(0, value.shape[0], lead)]
+    while shift < period // 2:
+        far, late = shift // lead, (delay & shift) != 0
+        padded = [blank] * far + tiles + [blank] * far
+        tiles = [jnp.where(late, padded[k], padded[k + far]) for k in range(len(tiles) + far)]
+        shift *= 2
+    half = shift // lead
+    tiles = tiles + [blank] * (2 * half - len(tiles))
+    upper = lax.broadcasted_iota(jnp.int32, (lead, LANES), 1) >= observers
+    late = ((delay & shift) != 0) != upper
+    tiles = [jnp.where(late, tiles[k + half], tiles[k]) for k in range(half)]
+    across = jnp.concatenate(tiles, axis=0).T
     rows = out_ref.shape[1]
     lane = lax.broadcasted_iota(jnp.int32, (per_device, LANES), 1)
     low = lane < steps
     for b in range(observers // per_device):
         for pair in range(period // LANES):
-            mine = value[b * per_device:(b + 1) * per_device, pair * LANES:(pair + 1) * LANES]
+            first = pair * observers + b * per_device
+            mine = across[first:first + per_device]
             turned = pltpu.roll(mine, steps, 1)
             if rows < per_device:
                 down = jnp.concatenate([mine[rows:], mine[:rows]], axis=0)
@@ -395,7 +410,7 @@
     projector = jnp.concatenate(
         [d1 * d1, d2 * d2, d3 * d3, 2.0 * d1 * d2, 2.0 * d1 * d3, 2.0 * d2 * d3], axis=0
     )
-    chunks = sources(projector, got, kept, weights[0], bins, blocks, slabs)
+    chunks = sources(projector, got, kept, weights[0], jnp.concatenate([bins.T] * 2, axis=1), blocks, slabs)
     chunks = lax.all_to_all(chunks, ("blk", "tm"), split_axis=0, concat_axis=0, tiled=True)
     return records(chunks, observers // blocks, steps)
 

time: 40.3 us -> 40 us (level)
    pallas_call x1, Pallas kernels: 1.52 us -> 1.02 us  [sources(): pl.pallas_call(functools.partial(last_kernel, slabs, per_device), out_sha...]
    all_to_all x1, blocking collectives: 11 us -> 11.4 us  [body(): lax.all_to_all(chunks, ('blk', 'tm'), split_axis=0, concat_axis=0, tiled=...]
where the time goes in v3:
time: 40 us; the launch traced here: 39.8 us
  Pallas kernels  12 us (30%)
  starting transfers between devices  11.7 us (29%)
  blocking collectives  11.4 us (28%)
  waiting for transfers between devices  4.04 us (10%)
  local copies, waits for them, and re-layouts  0.45 us (1%)
    ppermute x6, starting transfers between devices, swap(): lax.ppermute(values, 'blk', [(i, i ^ 1 << bit) for i in range(blocks)])  11.7 us
    all_to_all x1, blocking collectives, body(): lax.all_to_all(chunks, ('blk', 'tm'), split_axis=0, concat_axis=0, tiled=...  11.4 us
    pallas_call x2, Pallas kernels, stress_sums(): pl.pallas_call(functools.partial(stress_kernel, blocks, bits, leaving), o...  8.64 us
    ppermute x6, waiting for transfers between devices, swap(): lax.ppermute(values, 'blk', [(i, i ^ 1 << bit) for i in range(blocks)])  4.04 us
    pallas_call x1, Pallas kernels, sources(): pl.pallas_call(functools.partial(last_kernel, slabs, per_device), out_sha...  1.02 us
    pallas_call x1, Pallas kernels, sources(): pl.pallas_call(first_kernel, out_shape=jax.ShapeDtypeStruct((size // COMP...  0.86 us
  transfers between devices with their start and end apart: 6, of which 3 were waited for; matrix products, arithmetic and copies ran while one was open for 1% of the time, Pallas kernels for 13%

profile of v3, /device:TPU:0, one launch (start us, length us, event | category | flops | bytes accessed | tf_op | source)
XLA Modules:
  0.0 39.8 jit_solution(9602101170901061962)
XLA Ops:
  0.0 0.0 copy-start.2
  0.0 0.0 copy-start
  0.0 0.0 copy-start.3
  0.0 5.0 %leaving_sums.1 = (s16[784,128]{1,0:T(8,128)(2,1)}, s16[784,128]{1,0:T(8,128)(2,1)}) custom-call(s32[96]{0:T(128)} %bitcast.20, bf16[96,64,128]{2,1,0:T(8,128)(2,1)} %density_ref.3, bf16[96,4,64,128]{3,2,1,0:T(8,128)(2,1)} %flow_ref.3), custom_call_target="tpu_custom_call" | custom-call | tf_op jit(solution)/shard_map/leaving_sums/pallas_call | solution.py:181
  5.0 0.0 copy-start.4
  5.0 0.0 copy-start.1
  5.0 3.1 %collective-permute-start.3 = (s16[784,128]{1,0:T(8,128)(2,1)}, s16[784,128]{1,0:T(8,128)(2,1)S(1)}, u32[]{:S(2)}, u32[]{:S(2)}) collective-permute-start(s16[784,128]{1,0:T(8,128)(2,1)} %get-tuple-element.23), channel_id=1, source_target_pairs={{0,4},{4,0},{8,12},{12,8},{16,20},{20,16},{24,28},{28,24},{1,5},{5... | collective-permute-start | bytes 602120 | tf_op jit(solution)/shard_map/ppermute | solution.py:391
  8.2 1.4 %collective-permute-start = (s16[784,128]{1,0:T(8,128)(2,1)}, s16[784,128]{1,0:T(8,128)(2,1)S(1)}, u32[]{:S(2)}, u32[]{:S(2)}) collective-permute-start(s16[784,128]{1,0:T(8,128)(2,1)} %get-tuple-element.17), channel_id=1, source_target_pairs={{0,8},{4,12},{8,0},{12,4},{16,24},{20,28},{24,16},{28,20},{1,9},{5... | collective-permute-start | bytes 602120 | tf_op jit(solution)/shard_map/ppermute | solution.py:391
  9.6 0.0 copy-done.3
  9.6 0.0 copy-done.2
  9.6 0.0 copy-done
  9.6 3.6 %staying_sums.1 = (f32[768,128]{1,0:T(8,128)S(1)}, f32[768,128]{1,0:T(8,128)S(1)}) custom-call(s32[96]{0:T(128)S(1)} %bitcast.21, bf16[96,64,128]{2,1,0:T(8,128)(2,1)S(1)} %copy-done, bf16[96,4,64,128]{3,2,1,0:T(8,128)(2,1)} %flow_ref.3), custom_call_target="tpu_custom_call" | custom-call | tf_op jit(solution)/shard_map/staying_sums/pallas_call | solution.py:181
  13.2 0.1 broadcast_dynamic-update-slice_fusion.5
  13.3 0.1 broadcast_dynamic-update-slice_fusion.4
  13.4 0.1 broadcast_dynamic-update-slice_fusion.3
  13.5 0.1 broadcast_dynamic-update-slice_fusion.2
  13.5 0.1 broadcast_dynamic-update-slice_fusion.1
  13.6 0.0 collective-permute-done.3.refs_0_
  13.6 0.3 merge.6
  13.9 1.5 %collective-permute-start.4 = (s16[400,128]{1,0:T(8,128)(2,1)S(1)}, s16[400,128]{1,0:T(8,128)(2,1)S(1)}, u32[]{:S(2)}, u32[]{:S(2)}) collective-permute-start(s16[400,128]{1,0:T(8,128)(2,1)S(1)} %get-tuple-element.25), channel_id=1, source_target_pairs={{0,8},{4,12},{8,0},{12,4},{16,24},{20,28},{24,16},{28,20},{1,9},{5... | collective-permute-start | bytes 307208 | tf_op jit(solution)/shard_map/ppermute | solution.py:391
  15.4 0.0 collective-permute-done.refs_0_
  15.4 0.3 merge.4
  15.6 1.5 %collective-permute-start.1 = (s16[400,128]{1,0:T(8,128)(2,1)S(1)}, s16[400,128]{1,0:T(8,128)(2,1)S(1)}, u32[]{:S(2)}, u32[]{:S(2)}) collective-permute-start(s16[400,128]{1,0:T(8,128)(2,1)S(1)} %get-tuple-element.19), channel_id=1, source_target_pairs={{0,4},{4,0},{8,12},{12,8},{16,20},{20,16},{24,28},{28,24},{1,5},{5... | collective-permute-start | bytes 307208 | tf_op jit(solution)/shard_map/ppermute | solution.py:391
  17.2 0.1 broadcast_dynamic-update-slice_fusion.proj_ref
  17.2 1.4 %collective-permute-done.4.refs_0_ = s16[400,128]{1,0:T(8,128)(2,1)S(1)} collective-permute-done((s16[400,128]{1,0:T(8,128)(2,1)S(1)}, s16[400,128]{1,0:T(8,128)(2,1)S(1)}, u32[]{:S(2)}, u32[]{:S(2)}) %collective-permute-start.4) | collective-permute-done | bytes 102432 | tf_op jit(solution)/shard_map/ppermute | solution.py:391
  18.6 0.1 merge.7
  18.8 2.7 %collective-permute-start.5 = (s16[208,128]{1,0:T(8,128)(2,1)S(1)}, s16[208,128]{1,0:T(8,128)(2,1)S(1)}, u32[]{:S(2)}, u32[]{:S(2)}) collective-permute-start(s16[208,128]{1,0:T(8,128)(2,1)S(1)} %get-tuple-element.27), channel_id=1, source_target_pairs={{0,16},{4,20},{8,24},{12,28},{16,0},{20,4},{24,8},{28,12},{1,17},{... | collective-permute-start | bytes 159752 | tf_op jit(solution)/shard_map/ppermute | solution.py:391
  21.4 0.0 collective-permute-done.1.refs_0_
  21.4 0.1 merge.5
  21.6 1.5 %collective-permute-start.2 = (s16[208,128]{1,0:T(8,128)(2,1)S(1)}, s16[208,128]{1,0:T(8,128)(2,1)S(1)}, u32[]{:S(2)}, u32[]{:S(2)}) collective-permute-start(s16[208,128]{1,0:T(8,128)(2,1)S(1)} %get-tuple-element.21), channel_id=1, source_target_pairs={{0,16},{4,20},{8,24},{12,28},{16,0},{20,4},{24,8},{28,12},{1,17},{... | collective-permute-start | bytes 159752 | tf_op jit(solution)/shard_map/ppermute | solution.py:391
  23.1 0.0 copy-done.4
  23.1 0.1 pad_add_fusion.bins_ref
  23.2 2.1 %collective-permute-done.5.got_ref = s16[208,128]{1,0:T(8,128)(2,1)S(1)} collective-permute-done((s16[208,128]{1,0:T(8,128)(2,1)S(1)}, s16[208,128]{1,0:T(8,128)(2,1)S(1)}, u32[]{:S(2)}, u32[]{:S(2)}) %collective-permute-start.5) | collective-permute-done | bytes 53280 | tf_op jit(solution)/shard_map/ppermute | solution.py:391
  25.3 0.0 copy-done.1
  25.3 0.9 %first_sources.1.first_ref = f32[32,128]{1,0:T(8,128)S(1)} custom-call(f32[384,128]{1,0:T(8,128)S(1)} %broadcast_dynamic-update-slice_fusion.proj_ref, s16[208,128]{1,0:T(8,128)(2,1)S(1)} %collective-permute-done.5.got_ref, f32[192,128]{1,0:T(8,128)S(1)} %get-tuple-element.28.kept_ref, bf16[64,64,128]{2,1,0:T(8,128)(2,1)S(1)} %bitcast.18), custom_call_target="tpu_custom_call" | custom-call | tf_op jit(solution)/shard_map/first_sources/pallas_call | solution.py:343
  26.1 0.5 %collective-permute-done.2.got_ref = s16[208,128]{1,0:T(8,128)(2,1)S(1)} collective-permute-done((s16[208,128]{1,0:T(8,128)(2,1)S(1)}, s16[208,128]{1,0:T(8,128)(2,1)S(1)}, u32[]{:S(2)}, u32[]{:S(2)}) %collective-permute-start.2) | collective-permute-done | bytes 53280 | tf_op jit(solution)/shard_map/ppermute | solution.py:391
  26.7 1.0 %last_sources.1 = f32[32,4,128]{2,1,0:T(4,128)S(1)} custom-call(f32[384,128]{1,0:T(8,128)S(1)} %broadcast_dynamic-update-slice_fusion.proj_ref, s16[208,128]{1,0:T(8,128)(2,1)S(1)} %collective-permute-done.2.got_ref, f32[192,128]{1,0:T(8,128)S(1)} %get-tuple-element.22.kept_ref, bf16[64,64,128]{2,1,0:T(8,128)(2,1)S(1)} %bitcast.19, ...), custom_call_target="tpu_custom_call" | custom-call | tf_op jit(solution)/shard_map/last_sources/pallas_call | solution.py:352
  27.7 11.4 %all_to_all.5.got_ref = f32[32,4,128]{2,1,0:T(4,128)S(1)} all-to-all(f32[32,4,128]{2,1,0:T(4,128)S(1)} %last_sources.1), channel_id=1, replica_groups=mesh['blk'=8,'tm'=4] {'blk','tm'}, dimensions={0} | all-to-all | bytes 131072 | tf_op jit(solution)/shard_map/all_to_all | solution.py:414
  39.1 0.7 %records.1 = f32[8,64]{1,0:T(8,128)} custom-call(f32[32,4,128]{2,1,0:T(4,128)S(1)} %all_to_all.5.got_ref), custom_call_target="tpu_custom_call" | custom-call | tf_op jit(solution)/shard_map/records/pallas_call | solution.py:375
  (2 shorter events, 0.0 us)
Async XLA Ops:
  0.0 9.6 %copy-start.2 = (s32[96,1]{0,1:T(1,128)S(1)}, s32[96,1]{0,1:T(1,128)}, u32[]{:S(2)}) copy-start(s32[96,1]{0,1:T(1,128)} %param.8) | copy-start | bytes 1156
  0.0 9.6 %copy-start = (bf16[96,64,128]{2,1,0:T(8,128)(2,1)S(1)}, bf16[96,64,128]{2,1,0:T(8,128)(2,1)}, u32[]{:S(2)}) copy-start(bf16[96,64,128]{2,1,0:T(8,128)(2,1)} %density_ref.3) | copy-start | bytes 4718596
  0.0 9.5 %copy-start.3 = (f32[64,3]{0,1:T(4,128)S(1)}, f32[64,3]{0,1:T(4,128)}, u32[]{:S(2)}) copy-start(f32[64,3]{0,1:T(4,128)} %param.10) | copy-start | bytes 2308
  5.0 18.1 %copy-start.4 = (s32[64,1]{0,1:T(1,128)S(1)}, s32[64,1]{0,1:T(1,128)}, u32[]{:S(2)}) copy-start(s32[64,1]{0,1:T(1,128)} %param.11) | copy-start | bytes 772
  5.0 20.2 %copy-start.1 = (bf16[1,64,64,128]{3,2,1,0:T(8,128)(2,1)S(1)}, bf16[1,64,64,128]{3,2,1,0:T(8,128)(2,1)}, u32[]{:S(2)}) copy-start(bf16[1,64,64,128]{3,2,1,0:T(8,128)(2,1)} %param.9) | copy-start | bytes 3145732
  5.0 8.6 %collective-permute-start.3 = (s16[784,128]{1,0:T(8,128)(2,1)}, s16[784,128]{1,0:T(8,128)(2,1)S(1)}, u32[]{:S(2)}, u32[]{:S(2)}) collective-permute-start(s16[784,128]{1,0:T(8,128)(2,1)} %get-tuple-element.23), channel_id=1, source_target_pairs={{0,4},{4,0},{8,12},{12,8},{16,20},{20,16},{24,28},{28,24},{1,5},{5... | collective-permute-start | bytes 602120 | tf_op jit(solution)/shard_map/ppermute | solution.py:391
  8.2 7.2 %collective-permute-start = (s16[784,128]{1,0:T(8,128)(2,1)}, s16[784,128]{1,0:T(8,128)(2,1)S(1)}, u32[]{:S(2)}, u32[]{:S(2)}) collective-permute-start(s16[784,128]{1,0:T(8,128)(2,1)} %get-tuple-element.17), channel_id=1, source_target_pairs={{0,8},{4,12},{8,0},{12,4},{16,24},{20,28},{24,16},{28,20},{1,9},{5... | collective-permute-start | bytes 602120 | tf_op jit(solution)/shard_map/ppermute | solution.py:391
  13.9 4.7 %collective-permute-start.4 = (s16[400,128]{1,0:T(8,128)(2,1)S(1)}, s16[400,128]{1,0:T(8,128)(2,1)S(1)}, u32[]{:S(2)}, u32[]{:S(2)}) collective-permute-start(s16[400,128]{1,0:T(8,128)(2,1)S(1)} %get-tuple-element.25), channel_id=1, source_target_pairs={{0,8},{4,12},{8,0},{12,4},{16,24},{20,28},{24,16},{28,20},{1,9},{5... | collective-permute-start | bytes 307208 | tf_op jit(solution)/shard_map/ppermute | solution.py:391
  15.6 5.8 %collective-permute-start.1 = (s16[400,128]{1,0:T(8,128)(2,1)S(1)}, s16[400,128]{1,0:T(8,128)(2,1)S(1)}, u32[]{:S(2)}, u32[]{:S(2)}) collective-permute-start(s16[400,128]{1,0:T(8,128)(2,1)S(1)} %get-tuple-element.19), channel_id=1, source_target_pairs={{0,4},{4,0},{8,12},{12,8},{16,20},{20,16},{24,28},{28,24},{1,5},{5... | collective-permute-start | bytes 307208 | tf_op jit(solution)/shard_map/ppermute | solution.py:391
  18.8 6.5 %collective-permute-start.5 = (s16[208,128]{1,0:T(8,128)(2,1)S(1)}, s16[208,128]{1,0:T(8,128)(2,1)S(1)}, u32[]{:S(2)}, u32[]{:S(2)}) collective-permute-start(s16[208,128]{1,0:T(8,128)(2,1)S(1)} %get-tuple-element.27), channel_id=1, source_target_pairs={{0,16},{4,20},{8,24},{12,28},{16,0},{20,4},{24,8},{28,12},{1,17},{... | collective-permute-start | bytes 159752 | tf_op jit(solution)/shard_map/ppermute | solution.py:391
  21.6 5.1 %collective-permute-start.2 = (s16[208,128]{1,0:T(8,128)(2,1)S(1)}, s16[208,128]{1,0:T(8,128)(2,1)S(1)}, u32[]{:S(2)}, u32[]{:S(2)}) collective-permute-start(s16[208,128]{1,0:T(8,128)(2,1)S(1)} %get-tuple-element.21), channel_id=1, source_target_pairs={{0,16},{4,20},{8,24},{12,28},{16,0},{20,4},{24,8},{28,12},{1,17},{... | collective-permute-start | bytes 159752 | tf_op jit(solution)/shard_map/ppermute | solution.py:391

commit v4 on v3

--- a/solution.py
+++ b/solution.py
@@ -122,17 +122,16 @@
     return xx + excess, yy + excess, zz + excess, xy, xz, yz
 
 
-def stress_kernel(blocks, bits, leaving, dest_ref, density_ref, flow_ref, *refs):
-    halves = len(bits)
-    outs, (dens, flow, dest, counts, members, staged, sems, dest_sem) = refs[:halves], refs[halves:]
+def leaving_kernel(blocks, halves, dest_ref, density_ref, flow_ref, *refs):
+    sends, (dens, flow, counts, members) = refs[:halves], refs[halves:halves + 4]
+    dest, staged, sems, dest_sem = refs[halves + 4:]
     rows, steps = density_ref.shape[0], density_ref.shape[1]
-    tiles = steps // TILE
-    per_half = tiles // halves
+    per_half = steps // TILE // halves
     span = steps // halves
     fetch = pltpu.make_async_copy(dest_ref, dest, dest_sem)
     fetch.start()
     copies = []
-    for k in range(tiles):
+    for k in range(steps // TILE):
         at = pl.ds(k * TILE, TILE)
         pair = (
             pltpu.make_async_copy(density_ref.at[:, at, :], dens.at[pl.ds(0, rows), at, :], sems.at[k, 0]),
@@ -146,56 +145,81 @@
     flow[rows] = jnp.zeros_like(flow[rows])
     fetch.wait()
     bucket(blocks, rows, dest, counts, members)
-    me = lax.axis_index("blk")
     for half in range(halves):
-        target_ref = staged if leaving else outs[half]
         largest = jnp.zeros((TILE, LANES), jnp.float32)
         for k in range(per_half):
             tile = half * per_half + k
-            at = slice(tile * TILE, (tile + 1) * TILE)
             for copy in copies[tile]:
                 copy.wait()
 
             def block(i, top):
-                target = me ^ with_bit(i, bits[half], int(leaving))
-                pieces = block_sums(target, at, rows + UNROLL, dens, flow, counts, members)
+                pieces = slot_sums(half, i, 1, tile, dens, flow, counts, members)
                 for c, piece in enumerate(pieces):
-                    target_ref[rows_at((i * COMPS + c) * span + k * TILE), :] = piece
-                    if leaving:
-                        top = jnp.maximum(top, jnp.abs(piece))
+                    staged[rows_at((i * COMPS + c) * span + k * TILE), :] = piece
+                    top = jnp.maximum(top, jnp.abs(piece))
                 return top
 
             largest = lax.fori_loop(0, blocks // 2, block, largest)
-        if leaving:
-            write_codes(largest, staged, outs[half], blocks // 2 * COMPS * span)
-
-
-def stress_sums(density, flow_rest, targets, blocks, bits, leaving):
+        write_codes(largest, staged, sends[half], blocks // 2 * COMPS * span)
+
+
+def staying_kernel(blocks, halves, dens, flow, counts, members, *outs):
+    steps = dens.shape[1]
+    per_half = steps // TILE // halves
+    span = steps // halves
+    for half in range(halves):
+        for k in range(per_half):
+            def block(i, carry):
+                pieces = slot_sums(half, i, 0, half * per_half + k, dens, flow, counts, members)
+                for c, piece in enumerate(pieces):
+                    outs[half][rows_at((i * COMPS + c) * span + k * TILE), :] = piece
+                return carry
+
+            lax.fori_loop(0, blocks // 2, block, 0)
+
+
+def slot_sums(half, slot, leaving, tile, dens, flow, counts, members):
+    bit = half
+    target = lax.axis_index("blk") ^ with_bit(slot, bit, leaving)
+    at = slice(tile * TILE, (tile + 1) * TILE)
+    return block_sums(target, at, dens.shape[0] - 1 + UNROLL, dens, flow, counts, members)
+
+
+def leaving_sums(density, flow_rest, targets, blocks, halves):
     rows, steps, _ = density.shape
-    halves = len(bits)
     size = blocks // 2 * COMPS * (steps // halves)
-    if leaving:
-        out = jax.ShapeDtypeStruct((size + TILE, LANES), jnp.int16)
-    else:
-        out = jax.ShapeDtypeStruct((size, LANES), jnp.float32)
-    return pl.pallas_call(
-        functools.partial(stress_kernel, blocks, bits, leaving),
-        out_shape=[out] * halves,
-        in_specs=[pl.BlockSpec(memory_space=pl.ANY)] * 3,
-        out_specs=[whole()] * halves,
-        scratch_shapes=[
+    made = pl.pallas_call(
+        functools.partial(leaving_kernel, blocks, halves),
+        out_shape=[pltpu.VMEM((size + TILE, LANES), jnp.int16)] * halves + [
             pltpu.VMEM((rows + 1, steps, LANES), density.dtype),
             pltpu.VMEM((rows + 1, flow_rest.shape[1], steps, LANES), flow_rest.dtype),
-            pltpu.SMEM((rows,), jnp.int32),
             pltpu.SMEM((blocks,), jnp.int32),
             pltpu.SMEM((blocks * (rows + UNROLL),), jnp.int32),
-            pltpu.VMEM((size if leaving else TILE, LANES), jnp.float32),
+        ],
+        in_specs=[pl.BlockSpec(memory_space=pltpu.HBM)] * 3,
+        out_specs=[whole()] * (halves + 2) + [scalars()] * 2,
+        scratch_shapes=[
+            pltpu.SMEM((rows,), jnp.int32),
+            pltpu.VMEM((size, LANES), jnp.float32),
             pltpu.SemaphoreType.DMA((steps // TILE, 2)),
             pltpu.SemaphoreType.DMA(()),
         ],
-        compiler_params=params(58 if leaving else 50),
-        name="leaving_sums" if leaving else "staying_sums",
-    )(targets, density, flow_rest)
+        compiler_params=params(24),
+        name="leaving_sums",
+    )(pltpu.with_memory_space_constraint(targets, pltpu.HBM), pltpu.with_memory_space_constraint(density, pltpu.HBM), pltpu.with_memory_space_constraint(flow_rest, pltpu.HBM))
+    return list(made[:halves]), list(made[halves:])
+
+
+def staying_sums(held, blocks, halves):
+    size = blocks // 2 * COMPS * (held[0].shape[1] // halves)
+    return pl.pallas_call(
+        functools.partial(staying_kernel, blocks, halves),
+        out_shape=[jax.ShapeDtypeStruct((size, LANES), jnp.float32)] * halves,
+        in_specs=[whole()] * 2 + [scalars()] * 2,
+        out_specs=[whole()] * halves,
+        compiler_params=params(16),
+        name="staying_sums",
+    )(*held)
 
 
 def merge_kernel(count, positions, size, messages, *refs):
@@ -395,8 +419,8 @@
     orders[1][:2] = [1, 0]
     size = COMPS * (steps // 2)
     bits = tuple(order[0] for order in orders)
-    sends = stress_sums(density, flow_rest, dest[:, 0], blocks, bits, True)
-    kept = stress_sums(density, flow_rest, dest[:, 0], blocks, bits, False)
+    sends, held = leaving_sums(density, flow_rest, dest[:, 0], blocks, 2)
+    kept = staying_sums(held, blocks, 2)
     got = [swap(send, order[0]) for send, order in zip(sends, orders)]
     count = blocks // 2
     for stage in range(1, stages):

time: 40 us -> 38.9 us (0.972)
  Pallas kernels: 12 us -> 9.66 us
  starting transfers between devices: 11.7 us -> 12.8 us
    pallas_call x2, Pallas kernels: 8.64 us -> 6.34 us  [the longest x1 4.09 us: leaving_sums(): pl.pallas_call(functools.partial(leaving_kernel, blocks, halves), out_sha...]
    ppermute x6, starting transfers between devices: 11.7 us -> 12.8 us  [swap(): lax.ppermute(values, 'blk', [(i, i ^ 1 << bit) for i in range(blocks)])]
  transfers between devices with their start and end apart: 6 -> 6, of which waited for: 3 -> 4; matrix products, arithmetic and copies ran while one was open for 1% -> 1% of each run, Pallas kernels for 13% -> 10%
where the time goes in v4:
time: 38.9 us; the launch traced here: 38.8 us
  starting transfers between devices  12.8 us (33%)
  blocking collectives  11.7 us (30%)
  Pallas kernels  9.66 us (25%)
  waiting for transfers between devices  4.05 us (10%)
  local copies, waits for them, and re-layouts  0.44 us (1%)
    ppermute x6, starting transfers between devices, swap(): lax.ppermute(values, 'blk', [(i, i ^ 1 << bit) for i in range(blocks)])  12.8 us
    all_to_all x1, blocking collectives, body(): lax.all_to_all(chunks, ('blk', 'tm'), split_axis=0, concat_axis=0, tiled=...  11.7 us
    pallas_call x1, Pallas kernels, leaving_sums(): pl.pallas_call(functools.partial(leaving_kernel, blocks, halves), out_sha...  4.09 us
    ppermute x6, waiting for transfers between devices, swap(): lax.ppermute(values, 'blk', [(i, i ^ 1 << bit) for i in range(blocks)])  4.05 us
    pallas_call x1, Pallas kernels, staying_sums(): pl.pallas_call(functools.partial(staying_kernel, blocks, halves), out_sha...  2.25 us
    pallas_call x1, Pallas kernels, sources(): pl.pallas_call(functools.partial(last_kernel, slabs, per_device), out_sha...  1.02 us
    pallas_call x1, Pallas kernels, sources(): pl.pallas_call(first_kernel, out_shape=jax.ShapeDtypeStruct((size // COMP...  0.84 us
  transfers between devices with their start and end apart: 6, of which 4 were waited for; matrix products, arithmetic and copies ran while one was open for 1% of the time, Pallas kernels for 10%

profile of v4, /device:TPU:0, one launch (start us, length us, event | category | flops | bytes accessed | tf_op | source)
XLA Modules:
  0.0 38.8 jit_solution(17071194146790101189)
XLA Ops:
  0.0 0.0 copy-start.1
  0.0 4.1 %leaving_sums.1 = (s16[784,128]{1,0:T(8,128)(2,1)S(1)}, s16[784,128]{1,0:T(8,128)(2,1)S(1)}, bf16[97,64,128]{2,1,0:T(8,128)(2,1)S(1)}, bf16[97,4,64,128]{3,2,1,0...) custom-call(s32[96]{0:T(128)} %bitcast.20, bf16[96,64,128]{2,1,0:T(8,128)(2,1)} %density_ref.1, ...), custom_call_target="tpu_custom_call" | custom-call | tf_op jit(solution)/shard_map/leaving_sums/pallas_call | solution.py:191
  4.1 0.0 copy-start.2
  4.1 0.0 copy-start
  4.1 3.0 %collective-permute-start.3 = (s16[784,128]{1,0:T(8,128)(2,1)S(1)}, s16[784,128]{1,0:T(8,128)(2,1)S(1)}, u32[]{:S(2)}, u32[]{:S(2)}) collective-permute-start(s16[784,128]{1,0:T(8,128)(2,1)S(1)} %get-tuple-element.31), channel_id=1, source_target_pairs={{0,4},{4,0},{8,12},{12,8},{16,20},{20,16},{24,28},{28,24},{1,5},{5... | collective-permute-start | bytes 602120 | tf_op jit(solution)/shard_map/ppermute | solution.py:415
  7.1 1.6 %collective-permute-start = (s16[784,128]{1,0:T(8,128)(2,1)S(1)}, s16[784,128]{1,0:T(8,128)(2,1)S(1)}, u32[]{:S(2)}, u32[]{:S(2)}) collective-permute-start(s16[784,128]{1,0:T(8,128)(2,1)S(1)} %get-tuple-element.21), channel_id=1, source_target_pairs={{0,8},{4,12},{8,0},{12,4},{16,24},{20,28},{24,16},{28,20},{1,9},{5... | collective-permute-start | bytes 602120 | tf_op jit(solution)/shard_map/ppermute | solution.py:415
  8.7 0.0 copy-done.1
  8.8 0.1 broadcast_dynamic-update-slice_fusion.5
  8.8 0.1 broadcast_dynamic-update-slice_fusion.4
  8.9 0.1 broadcast_dynamic-update-slice_fusion.3
  9.0 0.1 broadcast_dynamic-update-slice_fusion.2
  9.0 2.2 %staying_sums.1 = (f32[768,128]{1,0:T(8,128)S(1)}, f32[768,128]{1,0:T(8,128)S(1)}) custom-call(bf16[97,64,128]{2,1,0:T(8,128)(2,1)S(1)} %get-tuple-element.22.dens, bf16[97,4,64,128]{3,2,1,0:T(8,128)(2,1)S(1)} %get-tuple-element.23.flow, s32[8]{0:T(128)S(4)} %get-tuple-element.24.counts, s32[800]{0:T(1024)S(4)} %get-tuple-element.25.members), custom_call_target="tpu_custom_call" | custom-call | tf_op jit(solution)/shard_map/staying_sums/pallas_call | solution.py:215
  11.3 0.1 broadcast_dynamic-update-slice_fusion.1
  11.4 0.7 %collective-permute-done.3.refs_0_ = s16[784,128]{1,0:T(8,128)(2,1)S(1)} collective-permute-done((s16[784,128]{1,0:T(8,128)(2,1)S(1)}, s16[784,128]{1,0:T(8,128)(2,1)S(1)}, u32[]{:S(2)}, u32[]{:S(2)}) %collective-permute-start.3) | collective-permute-done | bytes 200736 | tf_op jit(solution)/shard_map/ppermute | solution.py:415
  12.1 0.3 merge.6
  12.4 1.9 %collective-permute-start.4 = (s16[400,128]{1,0:T(8,128)(2,1)S(1)}, s16[400,128]{1,0:T(8,128)(2,1)S(1)}, u32[]{:S(2)}, u32[]{:S(2)}) collective-permute-start(s16[400,128]{1,0:T(8,128)(2,1)S(1)} %get-tuple-element.33), channel_id=1, source_target_pairs={{0,8},{4,12},{8,0},{12,4},{16,24},{20,28},{24,16},{28,20},{1,9},{5... | collective-permute-start | bytes 307208 | tf_op jit(solution)/shard_map/ppermute | solution.py:415
  14.3 0.0 collective-permute-done.refs_0_
  14.3 0.3 merge.4
  14.6 1.6 %collective-permute-start.1 = (s16[400,128]{1,0:T(8,128)(2,1)S(1)}, s16[400,128]{1,0:T(8,128)(2,1)S(1)}, u32[]{:S(2)}, u32[]{:S(2)}) collective-permute-start(s16[400,128]{1,0:T(8,128)(2,1)S(1)} %get-tuple-element.27), channel_id=1, source_target_pairs={{0,4},{4,0},{8,12},{12,8},{16,20},{20,16},{24,28},{28,24},{1,5},{5... | collective-permute-start | bytes 307208 | tf_op jit(solution)/shard_map/ppermute | solution.py:415
  16.1 0.1 broadcast_dynamic-update-slice_fusion.proj_ref
  16.2 0.9 %collective-permute-done.4.refs_0_ = s16[400,128]{1,0:T(8,128)(2,1)S(1)} collective-permute-done((s16[400,128]{1,0:T(8,128)(2,1)S(1)}, s16[400,128]{1,0:T(8,128)(2,1)S(1)}, u32[]{:S(2)}, u32[]{:S(2)}) %collective-permute-start.4) | collective-permute-done | bytes 102432 | tf_op jit(solution)/shard_map/ppermute | solution.py:415
  17.1 0.1 merge.7
  17.2 2.9 %collective-permute-start.5 = (s16[208,128]{1,0:T(8,128)(2,1)S(1)}, s16[208,128]{1,0:T(8,128)(2,1)S(1)}, u32[]{:S(2)}, u32[]{:S(2)}) collective-permute-start(s16[208,128]{1,0:T(8,128)(2,1)S(1)} %get-tuple-element.35), channel_id=1, source_target_pairs={{0,16},{4,20},{8,24},{12,28},{16,0},{20,4},{24,8},{28,12},{1,17},{... | collective-permute-start | bytes 159752 | tf_op jit(solution)/shard_map/ppermute | solution.py:415
  20.1 0.0 collective-permute-done.1.refs_0_
  20.1 0.1 merge.5
  20.3 1.8 %collective-permute-start.2 = (s16[208,128]{1,0:T(8,128)(2,1)S(1)}, s16[208,128]{1,0:T(8,128)(2,1)S(1)}, u32[]{:S(2)}, u32[]{:S(2)}) collective-permute-start(s16[208,128]{1,0:T(8,128)(2,1)S(1)} %get-tuple-element.29), channel_id=1, source_target_pairs={{0,16},{4,20},{8,24},{12,28},{16,0},{20,4},{24,8},{28,12},{1,17},{... | collective-permute-start | bytes 159752 | tf_op jit(solution)/shard_map/ppermute | solution.py:415
  22.1 0.0 copy-done.2
  22.1 0.1 pad_add_fusion.bins_ref
  22.1 1.5 %collective-permute-done.5.got_ref = s16[208,128]{1,0:T(8,128)(2,1)S(1)} collective-permute-done((s16[208,128]{1,0:T(8,128)(2,1)S(1)}, s16[208,128]{1,0:T(8,128)(2,1)S(1)}, u32[]{:S(2)}, u32[]{:S(2)}) %collective-permute-start.5) | collective-permute-done | bytes 53280 | tf_op jit(solution)/shard_map/ppermute | solution.py:415
  23.7 0.0 copy-done
  23.7 0.8 %first_sources.1.first_ref = f32[32,128]{1,0:T(8,128)S(1)} custom-call(f32[384,128]{1,0:T(8,128)S(1)} %broadcast_dynamic-update-slice_fusion.proj_ref, s16[208,128]{1,0:T(8,128)(2,1)S(1)} %collective-permute-done.5.got_ref, f32[192,128]{1,0:T(8,128)S(1)} %get-tuple-element.36.kept_ref, bf16[64,64,128]{2,1,0:T(8,128)(2,1)S(1)} %bitcast.18), custom_call_target="tpu_custom_call" | custom-call | tf_op jit(solution)/shard_map/first_sources/pallas_call | solution.py:367
  24.5 0.9 %collective-permute-done.2.got_ref = s16[208,128]{1,0:T(8,128)(2,1)S(1)} collective-permute-done((s16[208,128]{1,0:T(8,128)(2,1)S(1)}, s16[208,128]{1,0:T(8,128)(2,1)S(1)}, u32[]{:S(2)}, u32[]{:S(2)}) %collective-permute-start.2) | collective-permute-done | bytes 53280 | tf_op jit(solution)/shard_map/ppermute | solution.py:415
  25.4 1.0 %last_sources.1 = f32[32,4,128]{2,1,0:T(4,128)S(1)} custom-call(f32[384,128]{1,0:T(8,128)S(1)} %broadcast_dynamic-update-slice_fusion.proj_ref, s16[208,128]{1,0:T(8,128)(2,1)S(1)} %collective-permute-done.2.got_ref, f32[192,128]{1,0:T(8,128)S(1)} %get-tuple-element.30.kept_ref, bf16[64,64,128]{2,1,0:T(8,128)(2,1)S(1)} %bitcast.19, ...), custom_call_target="tpu_custom_call" | custom-call | tf_op jit(solution)/shard_map/last_sources/pallas_call | solution.py:376
  26.4 11.7 %all_to_all.5.got_ref = f32[32,4,128]{2,1,0:T(4,128)S(1)} all-to-all(f32[32,4,128]{2,1,0:T(4,128)S(1)} %last_sources.1), channel_id=1, replica_groups=mesh['blk'=8,'tm'=4] {'blk','tm'}, dimensions={0} | all-to-all | bytes 131072 | tf_op jit(solution)/shard_map/all_to_all | solution.py:438
  38.1 0.7 %records.1 = f32[8,64]{1,0:T(8,128)} custom-call(f32[32,4,128]{2,1,0:T(4,128)S(1)} %all_to_all.5.got_ref), custom_call_target="tpu_custom_call" | custom-call | tf_op jit(solution)/shard_map/records/pallas_call | solution.py:399
  (2 shorter events, 0.0 us)
Async XLA Ops:
  0.0 8.7 %copy-start.1 = (f32[64,3]{0,1:T(4,128)S(1)}, f32[64,3]{0,1:T(4,128)}, u32[]{:S(2)}) copy-start(f32[64,3]{0,1:T(4,128)} %param.10) | copy-start | bytes 2308
  4.1 18.0 %copy-start.2 = (s32[64,1]{0,1:T(1,128)S(1)}, s32[64,1]{0,1:T(1,128)}, u32[]{:S(2)}) copy-start(s32[64,1]{0,1:T(1,128)} %param.11) | copy-start | bytes 772
  4.1 19.5 %copy-start = (bf16[1,64,64,128]{3,2,1,0:T(8,128)(2,1)S(1)}, bf16[1,64,64,128]{3,2,1,0:T(8,128)(2,1)}, u32[]{:S(2)}) copy-start(bf16[1,64,64,128]{3,2,1,0:T(8,128)(2,1)} %param.9) | copy-start | bytes 3145732
  4.1 8.0 %collective-permute-start.3 = (s16[784,128]{1,0:T(8,128)(2,1)S(1)}, s16[784,128]{1,0:T(8,128)(2,1)S(1)}, u32[]{:S(2)}, u32[]{:S(2)}) collective-permute-start(s16[784,128]{1,0:T(8,128)(2,1)S(1)} %get-tuple-element.31), channel_id=1, source_target_pairs={{0,4},{4,0},{8,12},{12,8},{16,20},{20,16},{24,28},{28,24},{1,5},{5... | collective-permute-start | bytes 602120 | tf_op jit(solution)/shard_map/ppermute | solution.py:415
  7.1 7.2 %collective-permute-start = (s16[784,128]{1,0:T(8,128)(2,1)S(1)}, s16[784,128]{1,0:T(8,128)(2,1)S(1)}, u32[]{:S(2)}, u32[]{:S(2)}) collective-permute-start(s16[784,128]{1,0:T(8,128)(2,1)S(1)} %get-tuple-element.21), channel_id=1, source_target_pairs={{0,8},{4,12},{8,0},{12,4},{16,24},{20,28},{24,16},{28,20},{1,9},{5... | collective-permute-start | bytes 602120 | tf_op jit(solution)/shard_map/ppermute | solution.py:415
  12.4 4.7 %collective-permute-start.4 = (s16[400,128]{1,0:T(8,128)(2,1)S(1)}, s16[400,128]{1,0:T(8,128)(2,1)S(1)}, u32[]{:S(2)}, u32[]{:S(2)}) collective-permute-start(s16[400,128]{1,0:T(8,128)(2,1)S(1)} %get-tuple-element.33), channel_id=1, source_target_pairs={{0,8},{4,12},{8,0},{12,4},{16,24},{20,28},{24,16},{28,20},{1,9},{5... | collective-permute-start | bytes 307208 | tf_op jit(solution)/shard_map/ppermute | solution.py:415
  14.6 5.6 %collective-permute-start.1 = (s16[400,128]{1,0:T(8,128)(2,1)S(1)}, s16[400,128]{1,0:T(8,128)(2,1)S(1)}, u32[]{:S(2)}, u32[]{:S(2)}) collective-permute-start(s16[400,128]{1,0:T(8,128)(2,1)S(1)} %get-tuple-element.27), channel_id=1, source_target_pairs={{0,4},{4,0},{8,12},{12,8},{16,20},{20,16},{24,28},{28,24},{1,5},{5... | collective-permute-start | bytes 307208 | tf_op jit(solution)/shard_map/ppermute | solution.py:415
  17.2 6.4 %collective-permute-start.5 = (s16[208,128]{1,0:T(8,128)(2,1)S(1)}, s16[208,128]{1,0:T(8,128)(2,1)S(1)}, u32[]{:S(2)}, u32[]{:S(2)}) collective-permute-start(s16[208,128]{1,0:T(8,128)(2,1)S(1)} %get-tuple-element.35), channel_id=1, source_target_pairs={{0,16},{4,20},{8,24},{12,28},{16,0},{20,4},{24,8},{28,12},{1,17},{... | collective-permute-start | bytes 159752 | tf_op jit(solution)/shard_map/ppermute | solution.py:415
  20.3 5.1 %collective-permute-start.2 = (s16[208,128]{1,0:T(8,128)(2,1)S(1)}, s16[208,128]{1,0:T(8,128)(2,1)S(1)}, u32[]{:S(2)}, u32[]{:S(2)}) collective-permute-start(s16[208,128]{1,0:T(8,128)(2,1)S(1)} %get-tuple-element.29), channel_id=1, source_target_pairs={{0,16},{4,20},{8,24},{12,28},{16,0},{20,4},{24,8},{28,12},{1,17},{... | collective-permute-start | bytes 159752 | tf_op jit(solution)/shard_map/ppermute | solution.py:415

commit v5 on v4

--- a/solution.py
+++ b/solution.py
@@ -14,7 +14,7 @@
 UNROLL = 4
 GRAIN = 128.0
 TOP = 32764.0
-FLOOR = 1e-35
+FLOOR = 1e-33
 
 
 def whole():
@@ -222,56 +222,58 @@
     )(*held)
 
 
-def merge_kernel(count, positions, size, messages, *refs):
-    halves = len(positions)
-    got, kept = refs[:messages], refs[messages:messages + halves]
-    send, keeps, staged = refs[messages + halves], refs[messages + halves + 1:-1], refs[-1]
-    half = count // 2
-    largest = jnp.zeros((TILE, LANES), jnp.float32)
-    for p in range(halves):
-        message = got[min(p, messages - 1)]
-        offset = (p if messages < halves else 0) * count * size
-        factor = decode_factor(message[message.shape[0] - TILE:, :])
-
-        def total(block, k):
-            where = block * size + k * TILE
-            return kept[p][rows_at(where), :] + decode(message[rows_at(offset + where), :], factor)
-
-        def sent(i, top):
-            def tile(k, top):
-                piece = total(with_bit(i, positions[p], 1), k)
-                staged[rows_at((p * half + i) * size + k * TILE), :] = piece
-                return jnp.maximum(top, jnp.abs(piece))
-
-            return lax.fori_loop(0, size // TILE, tile, top, unroll=4)
-
-        largest = lax.fori_loop(0, half, sent, largest)
-
-        def stay(i, carry):
-            def tile(k, carry):
-                keeps[p][rows_at(i * size + k * TILE), :] = total(with_bit(i, positions[p], 0), k)
-                return carry
-
-            return lax.fori_loop(0, size // TILE, tile, carry, unroll=4)
-
-        lax.fori_loop(0, half, stay, 0)
-    write_codes(largest, staged, send, halves * half * size)
-
-
-def merge(got, kept, count, positions, size):
+def total_at(got, kept, factor, where):
+    return kept[rows_at(where), :] + decode(got[rows_at(where), :], factor)
+
+
+def send_kernel(count, position, size, got, kept, send, staged):
+    factor = decode_factor(got[count * size:count * size + TILE, :])
+
+    def block(i, top):
+        def tile(k, top):
+            piece = total_at(got, kept, factor, with_bit(i, position, 1) * size + k * TILE)
+            staged[rows_at(i * size + k * TILE), :] = piece
+            return jnp.maximum(top, jnp.abs(piece))
+
+        return lax.fori_loop(0, size // TILE, tile, top, unroll=4)
+
+    largest = lax.fori_loop(0, count // 2, block, jnp.zeros((TILE, LANES), jnp.float32))
+    write_codes(largest, staged, send, count // 2 * size)
+
+
+def keep_kernel(count, position, size, got, kept, keep):
+    factor = decode_factor(got[count * size:count * size + TILE, :])
+
+    def block(i, carry):
+        def tile(k, carry):
+            keep[rows_at(i * size + k * TILE), :] = total_at(got, kept, factor, with_bit(i, position, 0) * size + k * TILE)
+            return carry
+
+        return lax.fori_loop(0, size // TILE, tile, carry, unroll=4)
+
+    lax.fori_loop(0, count // 2, block, 0)
+
+
+def merge(got, kept, count, position, size):
     rows = count // 2 * size
-    halves = len(kept)
-    made = pl.pallas_call(
-        functools.partial(merge_kernel, count, tuple(positions), size, len(got)),
-        out_shape=[jax.ShapeDtypeStruct((halves * rows + TILE, LANES), jnp.int16)]
-        + [jax.ShapeDtypeStruct((rows, LANES), jnp.float32)] * halves,
-        in_specs=[whole()] * (len(got) + halves),
-        out_specs=[whole()] * (1 + halves),
-        scratch_shapes=[pltpu.VMEM((halves * rows, LANES), jnp.float32)],
+    send = pl.pallas_call(
+        functools.partial(send_kernel, count, position, size),
+        out_shape=jax.ShapeDtypeStruct((rows + TILE, LANES), jnp.int16),
+        in_specs=[whole()] * 2,
+        out_specs=whole(),
+        scratch_shapes=[pltpu.VMEM((rows, LANES), jnp.float32)],
         compiler_params=params(),
-        name="merge",
-    )(*got, *kept)
-    return made[0], list(made[1:])
+        name="merge_sent",
+    )(got, kept)
+    keep = pl.pallas_call(
+        functools.partial(keep_kernel, count, position, size),
+        out_shape=jax.ShapeDtypeStruct((rows, LANES), jnp.float32),
+        in_specs=[whole()] * 2,
+        out_specs=whole(),
+        compiler_params=params(),
+        name="merge_kept",
+    )(got, kept)
+    return send, keep
 
 
 def project(half, got_ref, kept_ref, proj_ref, weights_ref, totals):
@@ -425,9 +427,9 @@
     count = blocks // 2
     for stage in range(1, stages):
         places = [sorted(order[stage:]).index(order[stage]) for order in orders]
-        made = [merge(got[p:p + 1], kept[p:p + 1], count, places[p:p + 1], size) for p in range(2)]
+        made = [merge(got[p], kept[p], count, places[p], size) for p in range(2)]
         got = [swap(made[p][0], orders[p][stage]) for p in range(2)]
-        kept = made[0][1] + made[1][1]
+        kept = [made[p][1] for p in range(2)]
         count //= 2
 
     d1, d2, d3 = [jnp.broadcast_to(directions[:, c:c + 1], (observers, LANES)) for c in range(3)]

time: 38.9 us -> 38.8 us (level)
  starting transfers between devices: 12.8 us -> 12.4 us
    pallas_call x4 -> x8, Pallas kernels: 0.76 us -> 0.8 us  [the longest x4 0.53 us: merge(): pl.pallas_call(functools.partial(send_kernel, count, position, size), out...]
where the time goes in v5:
time: 38.8 us
  starting transfers between devices  12.4 us (32%)
  blocking collectives  11.8 us (30%)
  Pallas kernels  9.84 us (25%)
  waiting for transfers between devices  4.08 us (11%)
  local copies, waits for them, and re-layouts  0.44 us (1%)
    ppermute x6, starting transfers between devices, swap(): lax.ppermute(values, 'blk', [(i, i ^ 1 << bit) for i in range(blocks)])  12.4 us
    all_to_all x1, blocking collectives, body(): lax.all_to_all(chunks, ('blk', 'tm'), split_axis=0, concat_axis=0, tiled=...  11.8 us
    pallas_call x1, Pallas kernels, leaving_sums(): pl.pallas_call(functools.partial(leaving_kernel, blocks, halves), out_sha...  4.12 us
    ppermute x6, waiting for transfers between devices, swap(): lax.ppermute(values, 'blk', [(i, i ^ 1 << bit) for i in range(blocks)])  4.08 us
    pallas_call x1, Pallas kernels, staying_sums(): pl.pallas_call(functools.partial(staying_kernel, blocks, halves), out_sha...  2.37 us
    pallas_call x1, Pallas kernels, sources(): pl.pallas_call(functools.partial(last_kernel, slabs, per_device), out_sha...  1.02 us
    pallas_call x1, Pallas kernels, sources(): pl.pallas_call(first_kernel, out_shape=jax.ShapeDtypeStruct((size // COMP...  0.84 us
  transfers between devices with their start and end apart: 6, of which 4 were waited for; matrix products, arithmetic and copies ran while one was open for 1% of the time, Pallas kernels for 10%

profile of v5, /device:TPU:0, one launch (start us, length us, event | category | flops | bytes accessed | tf_op | source)
XLA Modules:
  0.0 38.8 jit_solution(12032355240934831932)
XLA Ops:
  0.0 0.0 copy-start.1
  0.0 4.1 %leaving_sums.1 = (s16[784,128]{1,0:T(8,128)(2,1)S(1)}, s16[784,128]{1,0:T(8,128)(2,1)S(1)}, bf16[97,64,128]{2,1,0:T(8,128)(2,1)S(1)}, bf16[97,4,64,128]{3,2,1,0...) custom-call(s32[96]{0:T(128)} %bitcast.20, bf16[96,64,128]{2,1,0:T(8,128)(2,1)} %density_ref.1, ...), custom_call_target="tpu_custom_call" | custom-call | tf_op jit(solution)/shard_map/leaving_sums/pallas_call | solution.py:191
  4.1 0.0 copy-start.2
  4.1 3.1 %collective-permute-start.3 = (s16[784,128]{1,0:T(8,128)(2,1)S(1)}, s16[784,128]{1,0:T(8,128)(2,1)S(1)}, u32[]{:S(2)}, u32[]{:S(2)}) collective-permute-start(s16[784,128]{1,0:T(8,128)(2,1)S(1)} %get-tuple-element.19), channel_id=1, source_target_pairs={{0,4},{4,0},{8,12},{12,8},{16,20},{20,16},{24,28},{28,24},{1,5},{5... | collective-permute-start | bytes 602120 | tf_op jit(solution)/shard_map/ppermute | solution.py:417
  7.3 1.4 %collective-permute-start = (s16[784,128]{1,0:T(8,128)(2,1)S(1)}, s16[784,128]{1,0:T(8,128)(2,1)S(1)}, u32[]{:S(2)}, u32[]{:S(2)}) collective-permute-start(s16[784,128]{1,0:T(8,128)(2,1)S(1)} %get-tuple-element.13), channel_id=1, source_target_pairs={{0,8},{4,12},{8,0},{12,4},{16,24},{20,28},{24,16},{28,20},{1,9},{5... | collective-permute-start | bytes 602120 | tf_op jit(solution)/shard_map/ppermute | solution.py:417
  8.7 0.0 copy-done.1
  8.7 0.1 broadcast_dynamic-update-slice_fusion.5
  8.8 0.1 broadcast_dynamic-update-slice_fusion.4
  8.9 0.0 copy-start
  8.9 0.1 broadcast_dynamic-update-slice_fusion.3
  8.9 0.1 broadcast_dynamic-update-slice_fusion.2
  9.0 2.4 %staying_sums.1 = (f32[768,128]{1,0:T(8,128)S(1)}, f32[768,128]{1,0:T(8,128)S(1)}) custom-call(bf16[97,64,128]{2,1,0:T(8,128)(2,1)S(1)} %get-tuple-element.14.dens, bf16[97,4,64,128]{3,2,1,0:T(8,128)(2,1)S(1)} %get-tuple-element.15.flow, s32[8]{0:T(128)S(4)} %get-tuple-element.16.counts, s32[800]{0:T(1024)S(4)} %get-tuple-element.17.members), custom_call_target="tpu_custom_call" | custom-call | tf_op jit(solution)/shard_map/staying_sums/pallas_call | solution.py:215
  11.4 0.1 broadcast_dynamic-update-slice_fusion.1
  11.5 0.8 %collective-permute-done.3.got = s16[784,128]{1,0:T(8,128)(2,1)S(1)} collective-permute-done((s16[784,128]{1,0:T(8,128)(2,1)S(1)}, s16[784,128]{1,0:T(8,128)(2,1)S(1)}, u32[]{:S(2)}, u32[]{:S(2)}) %collective-permute-start.3) | collective-permute-done | bytes 200736 | tf_op jit(solution)/shard_map/ppermute | solution.py:417
  12.3 0.2 merge_sent.6
  12.4 1.7 %collective-permute-start.4 = (s16[400,128]{1,0:T(8,128)(2,1)S(1)}, s16[400,128]{1,0:T(8,128)(2,1)S(1)}, u32[]{:S(2)}, u32[]{:S(2)}) collective-permute-start(s16[400,128]{1,0:T(8,128)(2,1)S(1)} %merge_sent.6), channel_id=1, source_target_pairs={{0,8},{4,12},{8,0},{12,4},{16,24},{20,28},{24,16},{28,20},{1,9},{5... | collective-permute-start | bytes 307208 | tf_op jit(solution)/shard_map/ppermute | solution.py:417
  14.1 0.0 collective-permute-done.got
  14.1 0.2 merge_sent.4
  14.3 1.6 %collective-permute-start.1 = (s16[400,128]{1,0:T(8,128)(2,1)S(1)}, s16[400,128]{1,0:T(8,128)(2,1)S(1)}, u32[]{:S(2)}, u32[]{:S(2)}) collective-permute-start(s16[400,128]{1,0:T(8,128)(2,1)S(1)} %merge_sent.4), channel_id=1, source_target_pairs={{0,4},{4,0},{8,12},{12,8},{16,20},{20,16},{24,28},{28,24},{1,5},{5... | collective-permute-start | bytes 307208 | tf_op jit(solution)/shard_map/ppermute | solution.py:417
  15.9 0.1 broadcast_dynamic-update-slice_fusion.proj_ref
  16.0 0.1 merge_kept.6.kept
  16.1 0.1 merge_kept.4.kept
  16.2 1.0 %collective-permute-done.4.got = s16[400,128]{1,0:T(8,128)(2,1)S(1)} collective-permute-done((s16[400,128]{1,0:T(8,128)(2,1)S(1)}, s16[400,128]{1,0:T(8,128)(2,1)S(1)}, u32[]{:S(2)}, u32[]{:S(2)}) %collective-permute-start.4) | collective-permute-done | bytes 102432 | tf_op jit(solution)/shard_map/ppermute | solution.py:417
  17.2 0.1 merge_sent.7
  17.3 2.8 %collective-permute-start.5 = (s16[208,128]{1,0:T(8,128)(2,1)S(1)}, s16[208,128]{1,0:T(8,128)(2,1)S(1)}, u32[]{:S(2)}, u32[]{:S(2)}) collective-permute-start(s16[208,128]{1,0:T(8,128)(2,1)S(1)} %merge_sent.7), channel_id=1, source_target_pairs={{0,16},{4,20},{8,24},{12,28},{16,0},{20,4},{24,8},{28,12},{1,17},{... | collective-permute-start | bytes 159752 | tf_op jit(solution)/shard_map/ppermute | solution.py:417
  20.0 0.0 collective-permute-done.1.got
  20.0 0.1 merge_sent.5
  20.1 1.8 %collective-permute-start.2 = (s16[208,128]{1,0:T(8,128)(2,1)S(1)}, s16[208,128]{1,0:T(8,128)(2,1)S(1)}, u32[]{:S(2)}, u32[]{:S(2)}) collective-permute-start(s16[208,128]{1,0:T(8,128)(2,1)S(1)} %merge_sent.5), channel_id=1, source_target_pairs={{0,16},{4,20},{8,24},{12,28},{16,0},{20,4},{24,8},{28,12},{1,17},{... | collective-permute-start | bytes 159752 | tf_op jit(solution)/shard_map/ppermute | solution.py:417
  21.9 0.0 copy-done.2
  21.9 0.1 pad_add_fusion.bins_ref
  22.1 0.3 collective-permute-done.5.got_ref
  22.4 0.0 copy-done
  22.4 0.8 %first_sources.1.first_ref = f32[32,128]{1,0:T(8,128)S(1)} custom-call(f32[384,128]{1,0:T(8,128)S(1)} %broadcast_dynamic-update-slice_fusion.proj_ref, s16[208,128]{1,0:T(8,128)(2,1)S(1)} %collective-permute-done.5.got_ref, f32[192,128]{1,0:T(8,128)S(1)} %merge_kept.7.kept_ref, bf16[64,64,128]{2,1,0:T(8,128)(2,1)S(1)} %bitcast.18), custom_call_target="tpu_custom_call" | custom-call | tf_op jit(solution)/shard_map/first_sources/pallas_call | solution.py:369
  23.3 2.0 %collective-permute-done.2.got_ref = s16[208,128]{1,0:T(8,128)(2,1)S(1)} collective-permute-done((s16[208,128]{1,0:T(8,128)(2,1)S(1)}, s16[208,128]{1,0:T(8,128)(2,1)S(1)}, u32[]{:S(2)}, u32[]{:S(2)}) %collective-permute-start.2) | collective-permute-done | bytes 53280 | tf_op jit(solution)/shard_map/ppermute | solution.py:417
  25.2 1.0 %last_sources.1 = f32[32,4,128]{2,1,0:T(4,128)S(1)} custom-call(f32[384,128]{1,0:T(8,128)S(1)} %broadcast_dynamic-update-slice_fusion.proj_ref, s16[208,128]{1,0:T(8,128)(2,1)S(1)} %collective-permute-done.2.got_ref, f32[192,128]{1,0:T(8,128)S(1)} %merge_kept.5.kept_ref, bf16[64,64,128]{2,1,0:T(8,128)(2,1)S(1)} %bitcast.19, ...), custom_call_target="tpu_custom_call" | custom-call | tf_op jit(solution)/shard_map/last_sources/pallas_call | solution.py:378
  26.3 11.8 %all_to_all.5.got_ref = f32[32,4,128]{2,1,0:T(4,128)S(1)} all-to-all(f32[32,4,128]{2,1,0:T(4,128)S(1)} %last_sources.1), channel_id=1, replica_groups=mesh['blk'=8,'tm'=4] {'blk','tm'}, dimensions={0} | all-to-all | bytes 131072 | tf_op jit(solution)/shard_map/all_to_all | solution.py:440
  38.1 0.7 %records.1 = f32[8,64]{1,0:T(8,128)} custom-call(f32[32,4,128]{2,1,0:T(4,128)S(1)} %all_to_all.5.got_ref), custom_call_target="tpu_custom_call" | custom-call | tf_op jit(solution)/shard_map/records/pallas_call | solution.py:401
  (4 shorter events, 0.1 us)
Async XLA Ops:
  0.0 8.7 %copy-start.1 = (f32[64,3]{0,1:T(4,128)S(1)}, f32[64,3]{0,1:T(4,128)}, u32[]{:S(2)}) copy-start(f32[64,3]{0,1:T(4,128)} %param.10) | copy-start | bytes 2308
  4.1 17.8 %copy-start.2 = (s32[64,1]{0,1:T(1,128)S(1)}, s32[64,1]{0,1:T(1,128)}, u32[]{:S(2)}) copy-start(s32[64,1]{0,1:T(1,128)} %param.11) | copy-start | bytes 772
  4.1 8.1 %collective-permute-start.3 = (s16[784,128]{1,0:T(8,128)(2,1)S(1)}, s16[784,128]{1,0:T(8,128)(2,1)S(1)}, u32[]{:S(2)}, u32[]{:S(2)}) collective-permute-start(s16[784,128]{1,0:T(8,128)(2,1)S(1)} %get-tuple-element.19), channel_id=1, source_target_pairs={{0,4},{4,0},{8,12},{12,8},{16,20},{20,16},{24,28},{28,24},{1,5},{5... | collective-permute-start | bytes 602120 | tf_op jit(solution)/shard_map/ppermute | solution.py:417
  7.3 6.8 %collective-permute-start = (s16[784,128]{1,0:T(8,128)(2,1)S(1)}, s16[784,128]{1,0:T(8,128)(2,1)S(1)}, u32[]{:S(2)}, u32[]{:S(2)}) collective-permute-start(s16[784,128]{1,0:T(8,128)(2,1)S(1)} %get-tuple-element.13), channel_id=1, source_target_pairs={{0,8},{4,12},{8,0},{12,4},{16,24},{20,28},{24,16},{28,20},{1,9},{5... | collective-permute-start | bytes 602120 | tf_op jit(solution)/shard_map/ppermute | solution.py:417
  8.9 13.5 %copy-start = (bf16[1,64,64,128]{3,2,1,0:T(8,128)(2,1)S(1)}, bf16[1,64,64,128]{3,2,1,0:T(8,128)(2,1)}, u32[]{:S(2)}) copy-start(bf16[1,64,64,128]{3,2,1,0:T(8,128)(2,1)} %param.9) | copy-start | bytes 3145732
  12.4 4.7 %collective-permute-start.4 = (s16[400,128]{1,0:T(8,128)(2,1)S(1)}, s16[400,128]{1,0:T(8,128)(2,1)S(1)}, u32[]{:S(2)}, u32[]{:S(2)}) collective-permute-start(s16[400,128]{1,0:T(8,128)(2,1)S(1)} %merge_sent.6), channel_id=1, source_target_pairs={{0,8},{4,12},{8,0},{12,4},{16,24},{20,28},{24,16},{28,20},{1,9},{5... | collective-permute-start | bytes 307208 | tf_op jit(solution)/shard_map/ppermute | solution.py:417
  14.3 5.7 %collective-permute-start.1 = (s16[400,128]{1,0:T(8,128)(2,1)S(1)}, s16[400,128]{1,0:T(8,128)(2,1)S(1)}, u32[]{:S(2)}, u32[]{:S(2)}) collective-permute-start(s16[400,128]{1,0:T(8,128)(2,1)S(1)} %merge_sent.4), channel_id=1, source_target_pairs={{0,4},{4,0},{8,12},{12,8},{16,20},{20,16},{24,28},{28,24},{1,5},{5... | collective-permute-start | bytes 307208 | tf_op jit(solution)/shard_map/ppermute | solution.py:417
  17.3 5.1 %collective-permute-start.5 = (s16[208,128]{1,0:T(8,128)(2,1)S(1)}, s16[208,128]{1,0:T(8,128)(2,1)S(1)}, u32[]{:S(2)}, u32[]{:S(2)}) collective-permute-start(s16[208,128]{1,0:T(8,128)(2,1)S(1)} %merge_sent.7), channel_id=1, source_target_pairs={{0,16},{4,20},{8,24},{12,28},{16,0},{20,4},{24,8},{28,12},{1,17},{... | collective-permute-start | bytes 159752 | tf_op jit(solution)/shard_map/ppermute | solution.py:417
  20.1 5.1 %collective-permute-start.2 = (s16[208,128]{1,0:T(8,128)(2,1)S(1)}, s16[208,128]{1,0:T(8,128)(2,1)S(1)}, u32[]{:S(2)}, u32[]{:S(2)}) collective-permute-start(s16[208,128]{1,0:T(8,128)(2,1)S(1)} %merge_sent.5), channel_id=1, source_target_pairs={{0,16},{4,20},{8,24},{12,28},{16,0},{20,4},{24,8},{28,12},{1,17},{... | collective-permute-start | bytes 159752 | tf_op jit(solution)/shard_map/ppermute | solution.py:417

commit v6 on v5

--- a/solution.py
+++ b/solution.py
@@ -68,7 +68,7 @@
         send_ref[where, :] = encode(staged[where, :], inverse)
         return carry
 
-    lax.fori_loop(0, rows // TILE, step, 0, unroll=4)
+    lax.fori_loop(0, rows // TILE, step, 0, unroll=8)
     send_ref[rows:rows + TILE, :] = code.astype(jnp.int32).astype(jnp.int16)
 
 
@@ -88,7 +88,7 @@
         counts[target] = count + 1
         return carry
 
-    lax.fori_loop(0, rows, place, 0, unroll=4)
+    lax.fori_loop(0, rows, place, 0, unroll=16)
 
     def pad(b, carry):
         end = b * stride + counts[b]
@@ -346,7 +346,8 @@
     rows = out_ref.shape[1]
     lane = lax.broadcasted_iota(jnp.int32, (per_device, LANES), 1)
     low = lane < steps
-    for b in range(observers // per_device):
+    blocks = observers // per_device
+    for b in range(blocks):
         for pair in range(period // LANES):
             first = pair * observers + b * per_device
             mine = across[first:first + per_device]
@@ -354,11 +355,11 @@
             if rows < per_device:
                 down = jnp.concatenate([mine[rows:], mine[:rows]], axis=0)
                 down_turned = jnp.concatenate([turned[rows:], turned[:rows]], axis=0)
-                out_ref[b * slabs + 2 * pair] = jnp.where(low, mine, down_turned)[:rows]
-                out_ref[b * slabs + 2 * pair + 1] = jnp.where(low, turned, down)[:rows]
+                out_ref[2 * pair * blocks + b] = jnp.where(low, mine, down_turned)[:rows]
+                out_ref[(2 * pair + 1) * blocks + b] = jnp.where(low, turned, down)[:rows]
             else:
-                out_ref[b * slabs + 2 * pair] = mine
-                out_ref[b * slabs + 2 * pair + 1] = turned
+                out_ref[2 * pair * blocks + b] = mine
+                out_ref[(2 * pair + 1) * blocks + b] = turned
 
 
 def sources(projector, got, kept, weights, bins, blocks, slabs):
@@ -437,7 +438,7 @@
         [d1 * d1, d2 * d2, d3 * d3, 2.0 * d1 * d2, 2.0 * d1 * d3, 2.0 * d2 * d3], axis=0
     )
     chunks = sources(projector, got, kept, weights[0], jnp.concatenate([bins.T] * 2, axis=1), blocks, slabs)
-    chunks = lax.all_to_all(chunks, ("blk", "tm"), split_axis=0, concat_axis=0, tiled=True)
+    chunks = lax.all_to_all(chunks, ("tm", "blk"), split_axis=0, concat_axis=0, tiled=True)
     return records(chunks, observers // blocks, steps)
 
 

time: 38.8 us -> 38.5 us (level)
  starting transfers between devices: 12.4 us -> 13.5 us
  waiting for transfers between devices: 4.08 us -> 3.23 us
  Pallas kernels: 9.84 us -> 9.45 us
    ppermute x6, starting transfers between devices: 12.4 us -> 13.5 us  [swap(): lax.ppermute(values, 'blk', [(i, i ^ 1 << bit) for i in range(blocks)])]
    ppermute x6, waiting for transfers between devices: 4.08 us -> 3.23 us  [swap(): lax.ppermute(values, 'blk', [(i, i ^ 1 << bit) for i in range(blocks)])]
where the time goes in v6:
time: 38.5 us; the launch traced here: 38.3 us
  starting transfers between devices  13.5 us (35%)
  blocking collectives  11.5 us (30%)
  Pallas kernels  9.45 us (25%)
  waiting for transfers between devices  3.23 us (8%)
  local copies, waits for them, and re-layouts  0.44 us (1%)
    ppermute x6, starting transfers between devices, swap(): lax.ppermute(values, 'blk', [(i, i ^ 1 << bit) for i in range(blocks)])  13.5 us
    all_to_all x1, blocking collectives, body(): lax.all_to_all(chunks, ('tm', 'blk'), split_axis=0, concat_axis=0, tiled=...  11.5 us
    pallas_call x1, Pallas kernels, leaving_sums(): pl.pallas_call(functools.partial(leaving_kernel, blocks, halves), out_sha...  4.05 us
    ppermute x6, waiting for transfers between devices, swap(): lax.ppermute(values, 'blk', [(i, i ^ 1 << bit) for i in range(blocks)])  3.23 us
    pallas_call x1, Pallas kernels, staying_sums(): pl.pallas_call(functools.partial(staying_kernel, blocks, halves), out_sha...  2.06 us
    pallas_call x1, Pallas kernels, sources(): pl.pallas_call(functools.partial(last_kernel, slabs, per_device), out_sha...  1.02 us
    pallas_call x1, Pallas kernels, sources(): pl.pallas_call(first_kernel, out_shape=jax.ShapeDtypeStruct((size // COMP...  0.84 us
  transfers between devices with their start and end apart: 6, of which 4 were waited for; matrix products, arithmetic and copies ran while one was open for 1% of the time, Pallas kernels for 10%

profile of v6, /device:TPU:0, one launch (start us, length us, event | category | flops | bytes accessed | tf_op | source)
XLA Modules:
  0.0 38.3 jit_solution(17853090038127366695)
XLA Ops:
  0.0 0.0 copy-start.1
  0.0 4.0 %leaving_sums.1 = (s16[784,128]{1,0:T(8,128)(2,1)S(1)}, s16[784,128]{1,0:T(8,128)(2,1)S(1)}, bf16[97,64,128]{2,1,0:T(8,128)(2,1)S(1)}, bf16[97,4,64,128]{3,2,1,0...) custom-call(s32[96]{0:T(128)} %bitcast.20, bf16[96,64,128]{2,1,0:T(8,128)(2,1)} %density_ref.1, ...), custom_call_target="tpu_custom_call" | custom-call | tf_op jit(solution)/shard_map/leaving_sums/pallas_call | solution.py:191
  4.1 0.0 copy-start.2
  4.1 3.0 %collective-permute-start.3 = (s16[784,128]{1,0:T(8,128)(2,1)S(1)}, s16[784,128]{1,0:T(8,128)(2,1)S(1)}, u32[]{:S(2)}, u32[]{:S(2)}) collective-permute-start(s16[784,128]{1,0:T(8,128)(2,1)S(1)} %get-tuple-element.19), channel_id=1, source_target_pairs={{0,4},{4,0},{8,12},{12,8},{16,20},{20,16},{24,28},{28,24},{1,5},{5... | collective-permute-start | bytes 602120 | tf_op jit(solution)/shard_map/ppermute | solution.py:418
  7.0 1.9 %collective-permute-start = (s16[784,128]{1,0:T(8,128)(2,1)S(1)}, s16[784,128]{1,0:T(8,128)(2,1)S(1)}, u32[]{:S(2)}, u32[]{:S(2)}) collective-permute-start(s16[784,128]{1,0:T(8,128)(2,1)S(1)} %get-tuple-element.13), channel_id=1, source_target_pairs={{0,8},{4,12},{8,0},{12,4},{16,24},{20,28},{24,16},{28,20},{1,9},{5... | collective-permute-start | bytes 602120 | tf_op jit(solution)/shard_map/ppermute | solution.py:418
  8.9 0.0 copy-done.1
  8.9 0.1 broadcast_dynamic-update-slice_fusion.5
  9.0 0.1 broadcast_dynamic-update-slice_fusion.4
  9.1 0.0 copy-start
  9.1 0.1 broadcast_dynamic-update-slice_fusion.3
  9.1 0.1 broadcast_dynamic-update-slice_fusion.2
  9.2 2.1 %staying_sums.1 = (f32[768,128]{1,0:T(8,128)S(1)}, f32[768,128]{1,0:T(8,128)S(1)}) custom-call(bf16[97,64,128]{2,1,0:T(8,128)(2,1)S(1)} %get-tuple-element.14.dens, bf16[97,4,64,128]{3,2,1,0:T(8,128)(2,1)S(1)} %get-tuple-element.15.flow, s32[8]{0:T(128)S(4)} %get-tuple-element.16.counts, s32[800]{0:T(1024)S(4)} %get-tuple-element.17.members), custom_call_target="tpu_custom_call" | custom-call | tf_op jit(solution)/shard_map/staying_sums/pallas_call | solution.py:215
  11.3 0.1 broadcast_dynamic-update-slice_fusion.1
  11.4 0.7 %collective-permute-done.3.got = s16[784,128]{1,0:T(8,128)(2,1)S(1)} collective-permute-done((s16[784,128]{1,0:T(8,128)(2,1)S(1)}, s16[784,128]{1,0:T(8,128)(2,1)S(1)}, u32[]{:S(2)}, u32[]{:S(2)}) %collective-permute-start.3) | collective-permute-done | bytes 200736 | tf_op jit(solution)/shard_map/ppermute | solution.py:418
  12.0 0.2 merge_sent.6
  12.2 2.2 %collective-permute-start.4 = (s16[400,128]{1,0:T(8,128)(2,1)S(1)}, s16[400,128]{1,0:T(8,128)(2,1)S(1)}, u32[]{:S(2)}, u32[]{:S(2)}) collective-permute-start(s16[400,128]{1,0:T(8,128)(2,1)S(1)} %merge_sent.6), channel_id=1, source_target_pairs={{0,8},{4,12},{8,0},{12,4},{16,24},{20,28},{24,16},{28,20},{1,9},{5... | collective-permute-start | bytes 307208 | tf_op jit(solution)/shard_map/ppermute | solution.py:418
  14.4 0.0 collective-permute-done.got
  14.4 0.2 merge_sent.4
  14.6 1.5 %collective-permute-start.1 = (s16[400,128]{1,0:T(8,128)(2,1)S(1)}, s16[400,128]{1,0:T(8,128)(2,1)S(1)}, u32[]{:S(2)}, u32[]{:S(2)}) collective-permute-start(s16[400,128]{1,0:T(8,128)(2,1)S(1)} %merge_sent.4), channel_id=1, source_target_pairs={{0,4},{4,0},{8,12},{12,8},{16,20},{20,16},{24,28},{28,24},{1,5},{5... | collective-permute-start | bytes 307208 | tf_op jit(solution)/shard_map/ppermute | solution.py:418
  16.1 0.1 broadcast_dynamic-update-slice_fusion.proj_ref
  16.2 0.1 merge_kept.6.kept
  16.3 0.1 merge_kept.4.kept
  16.4 0.6 %collective-permute-done.4.got = s16[400,128]{1,0:T(8,128)(2,1)S(1)} collective-permute-done((s16[400,128]{1,0:T(8,128)(2,1)S(1)}, s16[400,128]{1,0:T(8,128)(2,1)S(1)}, u32[]{:S(2)}, u32[]{:S(2)}) %collective-permute-start.4) | collective-permute-done | bytes 102432 | tf_op jit(solution)/shard_map/ppermute | solution.py:418
  17.0 0.1 merge_sent.7
  17.1 2.8 %collective-permute-start.5 = (s16[208,128]{1,0:T(8,128)(2,1)S(1)}, s16[208,128]{1,0:T(8,128)(2,1)S(1)}, u32[]{:S(2)}, u32[]{:S(2)}) collective-permute-start(s16[208,128]{1,0:T(8,128)(2,1)S(1)} %merge_sent.7), channel_id=1, source_target_pairs={{0,16},{4,20},{8,24},{12,28},{16,0},{20,4},{24,8},{28,12},{1,17},{... | collective-permute-start | bytes 159752 | tf_op jit(solution)/shard_map/ppermute | solution.py:418
  19.9 0.0 collective-permute-done.1.got
  19.9 0.1 merge_sent.5
  20.0 2.1 %collective-permute-start.2 = (s16[208,128]{1,0:T(8,128)(2,1)S(1)}, s16[208,128]{1,0:T(8,128)(2,1)S(1)}, u32[]{:S(2)}, u32[]{:S(2)}) collective-permute-start(s16[208,128]{1,0:T(8,128)(2,1)S(1)} %merge_sent.5), channel_id=1, source_target_pairs={{0,16},{4,20},{8,24},{12,28},{16,0},{20,4},{24,8},{28,12},{1,17},{... | collective-permute-start | bytes 159752 | tf_op jit(solution)/shard_map/ppermute | solution.py:418
  22.1 0.0 copy-done.2
  22.1 0.1 pad_add_fusion.bins_ref
  22.3 0.2 collective-permute-done.5.got_ref
  22.5 0.0 copy-done
  22.5 0.8 %first_sources.1.first_ref = f32[32,128]{1,0:T(8,128)S(1)} custom-call(f32[384,128]{1,0:T(8,128)S(1)} %broadcast_dynamic-update-slice_fusion.proj_ref, s16[208,128]{1,0:T(8,128)(2,1)S(1)} %collective-permute-done.5.got_ref, f32[192,128]{1,0:T(8,128)S(1)} %merge_kept.7.kept_ref, bf16[64,64,128]{2,1,0:T(8,128)(2,1)S(1)} %bitcast.18), custom_call_target="tpu_custom_call" | custom-call | tf_op jit(solution)/shard_map/first_sources/pallas_call | solution.py:370
  23.4 1.7 %collective-permute-done.2.got_ref = s16[208,128]{1,0:T(8,128)(2,1)S(1)} collective-permute-done((s16[208,128]{1,0:T(8,128)(2,1)S(1)}, s16[208,128]{1,0:T(8,128)(2,1)S(1)}, u32[]{:S(2)}, u32[]{:S(2)}) %collective-permute-start.2) | collective-permute-done | bytes 53280 | tf_op jit(solution)/shard_map/ppermute | solution.py:418
  25.1 1.0 %last_sources.1 = f32[32,4,128]{2,1,0:T(4,128)S(1)} custom-call(f32[384,128]{1,0:T(8,128)S(1)} %broadcast_dynamic-update-slice_fusion.proj_ref, s16[208,128]{1,0:T(8,128)(2,1)S(1)} %collective-permute-done.2.got_ref, f32[192,128]{1,0:T(8,128)S(1)} %merge_kept.5.kept_ref, bf16[64,64,128]{2,1,0:T(8,128)(2,1)S(1)} %bitcast.19, ...), custom_call_target="tpu_custom_call" | custom-call | tf_op jit(solution)/shard_map/last_sources/pallas_call | solution.py:379
  26.1 11.5 %all_to_all.5.got_ref = f32[32,4,128]{2,1,0:T(4,128)S(1)} all-to-all(f32[32,4,128]{2,1,0:T(4,128)S(1)} %last_sources.1), channel_id=1, replica_groups=mesh['blk'=8,'tm'=4] {'tm','blk'}, dimensions={0} | all-to-all | bytes 131072 | tf_op jit(solution)/shard_map/all_to_all | solution.py:441
  37.6 0.7 %records.1 = f32[8,64]{1,0:T(8,128)} custom-call(f32[32,4,128]{2,1,0:T(4,128)S(1)} %all_to_all.5.got_ref), custom_call_target="tpu_custom_call" | custom-call | tf_op jit(solution)/shard_map/records/pallas_call | solution.py:402
  (4 shorter events, 0.1 us)
Async XLA Ops:
  0.0 8.9 %copy-start.1 = (f32[64,3]{0,1:T(4,128)S(1)}, f32[64,3]{0,1:T(4,128)}, u32[]{:S(2)}) copy-start(f32[64,3]{0,1:T(4,128)} %param.10) | copy-start | bytes 2308
  4.1 18.1 %copy-start.2 = (s32[64,1]{0,1:T(1,128)S(1)}, s32[64,1]{0,1:T(1,128)}, u32[]{:S(2)}) copy-start(s32[64,1]{0,1:T(1,128)} %param.11) | copy-start | bytes 772
  4.1 7.9 %collective-permute-start.3 = (s16[784,128]{1,0:T(8,128)(2,1)S(1)}, s16[784,128]{1,0:T(8,128)(2,1)S(1)}, u32[]{:S(2)}, u32[]{:S(2)}) collective-permute-start(s16[784,128]{1,0:T(8,128)(2,1)S(1)} %get-tuple-element.19), channel_id=1, source_target_pairs={{0,4},{4,0},{8,12},{12,8},{16,20},{20,16},{24,28},{28,24},{1,5},{5... | collective-permute-start | bytes 602120 | tf_op jit(solution)/shard_map/ppermute | solution.py:418
  7.0 7.4 %collective-permute-start = (s16[784,128]{1,0:T(8,128)(2,1)S(1)}, s16[784,128]{1,0:T(8,128)(2,1)S(1)}, u32[]{:S(2)}, u32[]{:S(2)}) collective-permute-start(s16[784,128]{1,0:T(8,128)(2,1)S(1)} %get-tuple-element.13), channel_id=1, source_target_pairs={{0,8},{4,12},{8,0},{12,4},{16,24},{20,28},{24,16},{28,20},{1,9},{5... | collective-permute-start | bytes 602120 | tf_op jit(solution)/shard_map/ppermute | solution.py:418
  9.1 13.4 %copy-start = (bf16[1,64,64,128]{3,2,1,0:T(8,128)(2,1)S(1)}, bf16[1,64,64,128]{3,2,1,0:T(8,128)(2,1)}, u32[]{:S(2)}) copy-start(bf16[1,64,64,128]{3,2,1,0:T(8,128)(2,1)} %param.9) | copy-start | bytes 3145732
  12.2 4.8 %collective-permute-start.4 = (s16[400,128]{1,0:T(8,128)(2,1)S(1)}, s16[400,128]{1,0:T(8,128)(2,1)S(1)}, u32[]{:S(2)}, u32[]{:S(2)}) collective-permute-start(s16[400,128]{1,0:T(8,128)(2,1)S(1)} %merge_sent.6), channel_id=1, source_target_pairs={{0,8},{4,12},{8,0},{12,4},{16,24},{20,28},{24,16},{28,20},{1,9},{5... | collective-permute-start | bytes 307208 | tf_op jit(solution)/shard_map/ppermute | solution.py:418
  14.6 5.3 %collective-permute-start.1 = (s16[400,128]{1,0:T(8,128)(2,1)S(1)}, s16[400,128]{1,0:T(8,128)(2,1)S(1)}, u32[]{:S(2)}, u32[]{:S(2)}) collective-permute-start(s16[400,128]{1,0:T(8,128)(2,1)S(1)} %merge_sent.4), channel_id=1, source_target_pairs={{0,4},{4,0},{8,12},{12,8},{16,20},{20,16},{24,28},{28,24},{1,5},{5... | collective-permute-start | bytes 307208 | tf_op jit(solution)/shard_map/ppermute | solution.py:418
  17.1 5.4 %collective-permute-start.5 = (s16[208,128]{1,0:T(8,128)(2,1)S(1)}, s16[208,128]{1,0:T(8,128)(2,1)S(1)}, u32[]{:S(2)}, u32[]{:S(2)}) collective-permute-start(s16[208,128]{1,0:T(8,128)(2,1)S(1)} %merge_sent.7), channel_id=1, source_target_pairs={{0,16},{4,20},{8,24},{12,28},{16,0},{20,4},{24,8},{28,12},{1,17},{... | collective-permute-start | bytes 159752 | tf_op jit(solution)/shard_map/ppermute | solution.py:418
  20.0 5.1 %collective-permute-start.2 = (s16[208,128]{1,0:T(8,128)(2,1)S(1)}, s16[208,128]{1,0:T(8,128)(2,1)S(1)}, u32[]{:S(2)}, u32[]{:S(2)}) collective-permute-start(s16[208,128]{1,0:T(8,128)(2,1)S(1)} %merge_sent.5), channel_id=1, source_target_pairs={{0,16},{4,20},{8,24},{12,28},{16,0},{20,4},{24,8},{28,12},{1,17},{... | collective-permute-start | bytes 159752 | tf_op jit(solution)/shard_map/ppermute | solution.py:418

commit v7 on v6

--- a/solution.py
+++ b/solution.py
@@ -11,7 +11,7 @@
 TILE = 16
 LANES = 128
 GROUP = 8
-UNROLL = 4
+UNROLL = 6
 GRAIN = 128.0
 TOP = 32764.0
 FLOOR = 1e-33

time: 38.5 us -> 38.6 us (level)
  starting transfers between devices: 13.5 us -> 13.1 us
where the time goes in v7:
time: 38.6 us; the launch traced here: 38.3 us
  starting transfers between devices  13.1 us (34%)
  blocking collectives  11.5 us (30%)
  Pallas kernels  9.5 us (25%)
  waiting for transfers between devices  3.5 us (9%)
  local copies, waits for them, and re-layouts  0.44 us (1%)
    ppermute x6, starting transfers between devices, swap(): lax.ppermute(values, 'blk', [(i, i ^ 1 << bit) for i in range(blocks)])  13.1 us
    all_to_all x1, blocking collectives, body(): lax.all_to_all(chunks, ('tm', 'blk'), split_axis=0, concat_axis=0, tiled=...  11.5 us
    pallas_call x1, Pallas kernels, leaving_sums(): pl.pallas_call(functools.partial(leaving_kernel, blocks, halves), out_sha...  3.93 us
    ppermute x6, waiting for transfers between devices, swap(): lax.ppermute(values, 'blk', [(i, i ^ 1 << bit) for i in range(blocks)])  3.5 us
    pallas_call x1, Pallas kernels, staying_sums(): pl.pallas_call(functools.partial(staying_kernel, blocks, halves), out_sha...  2.23 us
    pallas_call x1, Pallas kernels, sources(): pl.pallas_call(functools.partial(last_kernel, slabs, per_device), out_sha...  1.02 us
    pallas_call x1, Pallas kernels, sources(): pl.pallas_call(first_kernel, out_shape=jax.ShapeDtypeStruct((size // COMP...  0.84 us
  transfers between devices with their start and end apart: 6, of which 4 were waited for; matrix products, arithmetic and copies ran while one was open for 1% of the time, Pallas kernels for 10%

profile of v7, /device:TPU:0, one launch (start us, length us, event | category | flops | bytes accessed | tf_op | source)
XLA Modules:
  0.0 38.3 jit_solution(1495214792501408576)
XLA Ops:
  0.0 0.0 copy-start.1
  0.0 3.9 %leaving_sums.1 = (s16[784,128]{1,0:T(8,128)(2,1)S(1)}, s16[784,128]{1,0:T(8,128)(2,1)S(1)}, bf16[97,64,128]{2,1,0:T(8,128)(2,1)S(1)}, bf16[97,4,64,128]{3,2,1,0...) custom-call(s32[96]{0:T(128)} %bitcast.20, bf16[96,64,128]{2,1,0:T(8,128)(2,1)} %density_ref.1, ...), custom_call_target="tpu_custom_call" | custom-call | tf_op jit(solution)/shard_map/leaving_sums/pallas_call | solution.py:191
  3.9 0.0 copy-start.2
  4.0 3.1 %collective-permute-start.3 = (s16[784,128]{1,0:T(8,128)(2,1)S(1)}, s16[784,128]{1,0:T(8,128)(2,1)S(1)}, u32[]{:S(2)}, u32[]{:S(2)}) collective-permute-start(s16[784,128]{1,0:T(8,128)(2,1)S(1)} %get-tuple-element.19), channel_id=1, source_target_pairs={{0,4},{4,0},{8,12},{12,8},{16,20},{20,16},{24,28},{28,24},{1,5},{5... | collective-permute-start | bytes 602120 | tf_op jit(solution)/shard_map/ppermute | solution.py:418
  7.1 1.7 %collective-permute-start = (s16[784,128]{1,0:T(8,128)(2,1)S(1)}, s16[784,128]{1,0:T(8,128)(2,1)S(1)}, u32[]{:S(2)}, u32[]{:S(2)}) collective-permute-start(s16[784,128]{1,0:T(8,128)(2,1)S(1)} %get-tuple-element.13), channel_id=1, source_target_pairs={{0,8},{4,12},{8,0},{12,4},{16,24},{20,28},{24,16},{28,20},{1,9},{5... | collective-permute-start | bytes 602120 | tf_op jit(solution)/shard_map/ppermute | solution.py:418
  8.8 0.0 copy-done.1
  8.8 0.1 broadcast_dynamic-update-slice_fusion.5
  8.9 0.1 broadcast_dynamic-update-slice_fusion.4
  8.9 0.0 copy-start
  8.9 0.1 broadcast_dynamic-update-slice_fusion.3
  9.0 0.1 broadcast_dynamic-update-slice_fusion.2
  9.1 2.2 %staying_sums.1 = (f32[768,128]{1,0:T(8,128)S(1)}, f32[768,128]{1,0:T(8,128)S(1)}) custom-call(bf16[97,64,128]{2,1,0:T(8,128)(2,1)S(1)} %get-tuple-element.14.dens, bf16[97,4,64,128]{3,2,1,0:T(8,128)(2,1)S(1)} %get-tuple-element.15.flow, s32[8]{0:T(128)S(4)} %get-tuple-element.16.counts, s32[816]{0:T(1024)S(4)} %get-tuple-element.17.members), custom_call_target="tpu_custom_call" | custom-call | tf_op jit(solution)/shard_map/staying_sums/pallas_call | solution.py:215
  11.3 0.1 broadcast_dynamic-update-slice_fusion.1
  11.4 0.7 %collective-permute-done.3.got = s16[784,128]{1,0:T(8,128)(2,1)S(1)} collective-permute-done((s16[784,128]{1,0:T(8,128)(2,1)S(1)}, s16[784,128]{1,0:T(8,128)(2,1)S(1)}, u32[]{:S(2)}, u32[]{:S(2)}) %collective-permute-start.3) | collective-permute-done | bytes 200736 | tf_op jit(solution)/shard_map/ppermute | solution.py:418
  12.1 0.2 merge_sent.6
  12.2 2.0 %collective-permute-start.4 = (s16[400,128]{1,0:T(8,128)(2,1)S(1)}, s16[400,128]{1,0:T(8,128)(2,1)S(1)}, u32[]{:S(2)}, u32[]{:S(2)}) collective-permute-start(s16[400,128]{1,0:T(8,128)(2,1)S(1)} %merge_sent.6), channel_id=1, source_target_pairs={{0,8},{4,12},{8,0},{12,4},{16,24},{20,28},{24,16},{28,20},{1,9},{5... | collective-permute-start | bytes 307208 | tf_op jit(solution)/shard_map/ppermute | solution.py:418
  14.2 0.0 collective-permute-done.got
  14.2 0.2 merge_sent.4
  14.4 1.6 %collective-permute-start.1 = (s16[400,128]{1,0:T(8,128)(2,1)S(1)}, s16[400,128]{1,0:T(8,128)(2,1)S(1)}, u32[]{:S(2)}, u32[]{:S(2)}) collective-permute-start(s16[400,128]{1,0:T(8,128)(2,1)S(1)} %merge_sent.4), channel_id=1, source_target_pairs={{0,4},{4,0},{8,12},{12,8},{16,20},{20,16},{24,28},{28,24},{1,5},{5... | collective-permute-start | bytes 307208 | tf_op jit(solution)/shard_map/ppermute | solution.py:418
  16.0 0.1 broadcast_dynamic-update-slice_fusion.proj_ref
  16.0 0.1 merge_kept.6.kept
  16.1 0.1 merge_kept.4.kept
  16.2 0.7 %collective-permute-done.4.got = s16[400,128]{1,0:T(8,128)(2,1)S(1)} collective-permute-done((s16[400,128]{1,0:T(8,128)(2,1)S(1)}, s16[400,128]{1,0:T(8,128)(2,1)S(1)}, u32[]{:S(2)}, u32[]{:S(2)}) %collective-permute-start.4) | collective-permute-done | bytes 102432 | tf_op jit(solution)/shard_map/ppermute | solution.py:418
  17.0 0.1 merge_sent.7
  17.1 2.8 %collective-permute-start.5 = (s16[208,128]{1,0:T(8,128)(2,1)S(1)}, s16[208,128]{1,0:T(8,128)(2,1)S(1)}, u32[]{:S(2)}, u32[]{:S(2)}) collective-permute-start(s16[208,128]{1,0:T(8,128)(2,1)S(1)} %merge_sent.7), channel_id=1, source_target_pairs={{0,16},{4,20},{8,24},{12,28},{16,0},{20,4},{24,8},{28,12},{1,17},{... | collective-permute-start | bytes 159752 | tf_op jit(solution)/shard_map/ppermute | solution.py:418
  19.8 0.0 collective-permute-done.1.got
  19.9 0.1 merge_sent.5
  20.0 2.0 %collective-permute-start.2 = (s16[208,128]{1,0:T(8,128)(2,1)S(1)}, s16[208,128]{1,0:T(8,128)(2,1)S(1)}, u32[]{:S(2)}, u32[]{:S(2)}) collective-permute-start(s16[208,128]{1,0:T(8,128)(2,1)S(1)} %merge_sent.5), channel_id=1, source_target_pairs={{0,16},{4,20},{8,24},{12,28},{16,0},{20,4},{24,8},{28,12},{1,17},{... | collective-permute-start | bytes 159752 | tf_op jit(solution)/shard_map/ppermute | solution.py:418
  21.9 0.0 copy-done.2
  21.9 0.1 pad_add_fusion.bins_ref
  22.1 0.2 collective-permute-done.5.got_ref
  22.3 0.0 copy-done
  22.3 0.8 %first_sources.1.first_ref = f32[32,128]{1,0:T(8,128)S(1)} custom-call(f32[384,128]{1,0:T(8,128)S(1)} %broadcast_dynamic-update-slice_fusion.proj_ref, s16[208,128]{1,0:T(8,128)(2,1)S(1)} %collective-permute-done.5.got_ref, f32[192,128]{1,0:T(8,128)S(1)} %merge_kept.7.kept_ref, bf16[64,64,128]{2,1,0:T(8,128)(2,1)S(1)} %bitcast.18), custom_call_target="tpu_custom_call" | custom-call | tf_op jit(solution)/shard_map/first_sources/pallas_call | solution.py:370
  23.2 1.9 %collective-permute-done.2.got_ref = s16[208,128]{1,0:T(8,128)(2,1)S(1)} collective-permute-done((s16[208,128]{1,0:T(8,128)(2,1)S(1)}, s16[208,128]{1,0:T(8,128)(2,1)S(1)}, u32[]{:S(2)}, u32[]{:S(2)}) %collective-permute-start.2) | collective-permute-done | bytes 53280 | tf_op jit(solution)/shard_map/ppermute | solution.py:418
  25.1 1.0 %last_sources.1 = f32[32,4,128]{2,1,0:T(4,128)S(1)} custom-call(f32[384,128]{1,0:T(8,128)S(1)} %broadcast_dynamic-update-slice_fusion.proj_ref, s16[208,128]{1,0:T(8,128)(2,1)S(1)} %collective-permute-done.2.got_ref, f32[192,128]{1,0:T(8,128)S(1)} %merge_kept.5.kept_ref, bf16[64,64,128]{2,1,0:T(8,128)(2,1)S(1)} %bitcast.19, ...), custom_call_target="tpu_custom_call" | custom-call | tf_op jit(solution)/shard_map/last_sources/pallas_call | solution.py:379
  26.1 11.5 %all_to_all.5.got_ref = f32[32,4,128]{2,1,0:T(4,128)S(1)} all-to-all(f32[32,4,128]{2,1,0:T(4,128)S(1)} %last_sources.1), channel_id=1, replica_groups=mesh['blk'=8,'tm'=4] {'tm','blk'}, dimensions={0} | all-to-all | bytes 131072 | tf_op jit(solution)/shard_map/all_to_all | solution.py:441
  37.6 0.7 %records.1 = f32[8,64]{1,0:T(8,128)} custom-call(f32[32,4,128]{2,1,0:T(4,128)S(1)} %all_to_all.5.got_ref), custom_call_target="tpu_custom_call" | custom-call | tf_op jit(solution)/shard_map/records/pallas_call | solution.py:402
  (4 shorter events, 0.1 us)
Async XLA Ops:
  0.0 8.8 %copy-start.1 = (f32[64,3]{0,1:T(4,128)S(1)}, f32[64,3]{0,1:T(4,128)}, u32[]{:S(2)}) copy-start(f32[64,3]{0,1:T(4,128)} %param.10) | copy-start | bytes 2308
  3.9 18.0 %copy-start.2 = (s32[64,1]{0,1:T(1,128)S(1)}, s32[64,1]{0,1:T(1,128)}, u32[]{:S(2)}) copy-start(s32[64,1]{0,1:T(1,128)} %param.11) | copy-start | bytes 772
  4.0 8.1 %collective-permute-start.3 = (s16[784,128]{1,0:T(8,128)(2,1)S(1)}, s16[784,128]{1,0:T(8,128)(2,1)S(1)}, u32[]{:S(2)}, u32[]{:S(2)}) collective-permute-start(s16[784,128]{1,0:T(8,128)(2,1)S(1)} %get-tuple-element.19), channel_id=1, source_target_pairs={{0,4},{4,0},{8,12},{12,8},{16,20},{20,16},{24,28},{28,24},{1,5},{5... | collective-permute-start | bytes 602120 | tf_op jit(solution)/shard_map/ppermute | solution.py:418
  7.1 7.1 %collective-permute-start = (s16[784,128]{1,0:T(8,128)(2,1)S(1)}, s16[784,128]{1,0:T(8,128)(2,1)S(1)}, u32[]{:S(2)}, u32[]{:S(2)}) collective-permute-start(s16[784,128]{1,0:T(8,128)(2,1)S(1)} %get-tuple-element.13), channel_id=1, source_target_pairs={{0,8},{4,12},{8,0},{12,4},{16,24},{20,28},{24,16},{28,20},{1,9},{5... | collective-permute-start | bytes 602120 | tf_op jit(solution)/shard_map/ppermute | solution.py:418
  8.9 13.4 %copy-start = (bf16[1,64,64,128]{3,2,1,0:T(8,128)(2,1)S(1)}, bf16[1,64,64,128]{3,2,1,0:T(8,128)(2,1)}, u32[]{:S(2)}) copy-start(bf16[1,64,64,128]{3,2,1,0:T(8,128)(2,1)} %param.9) | copy-start | bytes 3145732
  12.2 4.7 %collective-permute-start.4 = (s16[400,128]{1,0:T(8,128)(2,1)S(1)}, s16[400,128]{1,0:T(8,128)(2,1)S(1)}, u32[]{:S(2)}, u32[]{:S(2)}) collective-permute-start(s16[400,128]{1,0:T(8,128)(2,1)S(1)} %merge_sent.6), channel_id=1, source_target_pairs={{0,8},{4,12},{8,0},{12,4},{16,24},{20,28},{24,16},{28,20},{1,9},{5... | collective-permute-start | bytes 307208 | tf_op jit(solution)/shard_map/ppermute | solution.py:418
  14.4 5.5 %collective-permute-start.1 = (s16[400,128]{1,0:T(8,128)(2,1)S(1)}, s16[400,128]{1,0:T(8,128)(2,1)S(1)}, u32[]{:S(2)}, u32[]{:S(2)}) collective-permute-start(s16[400,128]{1,0:T(8,128)(2,1)S(1)} %merge_sent.4), channel_id=1, source_target_pairs={{0,4},{4,0},{8,12},{12,8},{16,20},{20,16},{24,28},{28,24},{1,5},{5... | collective-permute-start | bytes 307208 | tf_op jit(solution)/shard_map/ppermute | solution.py:418
  17.1 5.2 %collective-permute-start.5 = (s16[208,128]{1,0:T(8,128)(2,1)S(1)}, s16[208,128]{1,0:T(8,128)(2,1)S(1)}, u32[]{:S(2)}, u32[]{:S(2)}) collective-permute-start(s16[208,128]{1,0:T(8,128)(2,1)S(1)} %merge_sent.7), channel_id=1, source_target_pairs={{0,16},{4,20},{8,24},{12,28},{16,0},{20,4},{24,8},{28,12},{1,17},{... | collective-permute-start | bytes 159752 | tf_op jit(solution)/shard_map/ppermute | solution.py:418
  20.0 5.1 %collective-permute-start.2 = (s16[208,128]{1,0:T(8,128)(2,1)S(1)}, s16[208,128]{1,0:T(8,128)(2,1)S(1)}, u32[]{:S(2)}, u32[]{:S(2)}) collective-permute-start(s16[208,128]{1,0:T(8,128)(2,1)S(1)} %merge_sent.5), channel_id=1, source_target_pairs={{0,16},{4,20},{8,24},{12,28},{16,0},{20,4},{24,8},{28,12},{1,17},{... | collective-permute-start | bytes 159752 | tf_op jit(solution)/shard_map/ppermute | solution.py:418
